TPU v7x, 512 devices: a whole 4x8x8 slice. The times are simulated.
512 devices in a mesh: dp: 64 (over x, y, core), fsdp: 8 (over z).
Axes of the slice: x: 4, y: 8, z: 8, core: 2. Of those that a mesh axis runs over, the one named last changes fastest.
Arguments:
- frames: bfloat16 [131072, 1536], P(('dp', 'fsdp')), may hold values from -100 to 100
- destination: int32 [32768], P(('dp', 'fsdp')), may hold values from 0 to 4095, as said below
- utt_lengths: int32 [512, 4], P(('dp', 'fsdp')), may hold values from 1 to 128, 256 in all within a row
- cotangent: bfloat16 [131072, 1536], P(('dp', 'fsdp')), may hold values from -24 to 24
- weight: bfloat16 [1536, 1536], P('fsdp'), may hold values from -0.15625 to 0.15625
- kernel: float32 [31, 1536], replicated, may hold values from -1 to 1
- norm_gain: float32 [1536], replicated, may hold values from 0.1 to 1.9
- norm_shift: float32 [1536], replicated, may hold values from -3 to 3
Outputs:
- grad_input: bfloat16 [131072, 1536], P(('dp', 'fsdp'))
- grad_weight: float32 [1536, 1536], P('fsdp')
- grad_kernel: float32 [31, 1536], replicated
- grad_gain: float32 [1536], replicated
- grad_shift: float32 [1536], replicated
Inputs may be any that keep to these rules, and one draw needn't show every extreme that they name: `destination`: within one fsdp index the entries of all devices are each of 0 to 4095 once. The 64 blocks of one device go to exactly 64 owners, 1 block to each.
All inputs are finite; a program needn't handle non-finite values.
Results may differ from a plain program's by a relative error of at most 0.0065.
Values may be sent and summed in bfloat16 or wider, within the bound.
A program may use at most 128 MiB of HBM per device.

v0:
```python
import math

import jax
import jax.numpy as jnp
from jax import lax
from jax.sharding import PartitionSpec as P

EPSILON = 1e-05


def segment_ids(lengths, row_count):
    utt_ends = jnp.cumsum(lengths)
    positions = jnp.arange(row_count, dtype=jnp.int32)
    return jnp.sum((positions[:, None] >= utt_ends[None, :]).astype(jnp.int32), axis=1)


def on_device(frames, destination, utt_lengths, cotangent, weight, kernel, norm_gain, norm_shift):
    dp_size = lax.axis_size("dp")
    fsdp_size = lax.axis_size("fsdp")
    block_count = destination.shape[0]
    row_count = frames.shape[0]
    block_rows = row_count // block_count
    channels = frames.shape[1]
    spread = min(block_count, dp_size)
    capacity = block_count // spread
    dest_owner = destination // block_count
    dest_slot = destination % block_count
    block_index = jnp.arange(block_count, dtype=jnp.int32)
    same_owner = (dest_owner[:, None] == dest_owner[None, :]) & (
        block_index[None, :] < block_index[:, None]
    )
    peer_rank = jnp.sum(same_owner.astype(jnp.int32), axis=1)
    send_place = dest_owner * capacity + peer_rank
    pieces = frames.reshape(block_count, block_rows, channels)
    outgoing = (
        jnp.zeros((dp_size * capacity, block_rows, channels), jnp.bfloat16)
        .at[send_place]
        .set(pieces)
    )
    outgoing = outgoing.reshape(dp_size, capacity, block_rows, channels)
    labels = (
        jnp.full((dp_size * capacity,), -1, jnp.int32)
        .at[send_place]
        .set(dest_slot)
        .reshape(dp_size, capacity)
    )
    arrived, arrived_slot = (
        lax.all_to_all(outgoing, "dp", split_axis=0, concat_axis=0, tiled=True),
        lax.all_to_all(labels, "dp", split_axis=0, concat_axis=0, tiled=True),
    )
    flat_slot = arrived_slot.reshape(-1)
    recv_target = jnp.where(flat_slot < 0, block_count, flat_slot)
    local_frames = jnp.zeros((block_count + 1, block_rows, channels), jnp.bfloat16)
    local_frames = local_frames.at[recv_target].set(arrived.reshape(-1, block_rows, channels))
    local_frames = local_frames[:block_count].reshape(row_count, channels)
    grad_hidden = jnp.dot(
        cotangent,
        lax.all_gather(weight, "fsdp", axis=0, tiled=True),
        preferred_element_type=jnp.float32,
    )
    tap_count = kernel.shape[0]
    half_taps = tap_count // 2
    segment = segment_ids(utt_lengths[0], row_count)
    segment_pad = jnp.pad(segment, half_taps, constant_values=-1)
    signal = local_frames.astype(jnp.float32)
    signal_pad = jnp.pad(signal, ((half_taps, half_taps), (0, 0)))
    filtered = jnp.zeros_like(signal)
    for offset in range(tap_count):
        inside = (segment_pad[offset : offset + row_count] == segment).astype(jnp.float32)[:, None]
        filtered = filtered + kernel[offset] * signal_pad[offset : offset + row_count] * inside
    centered = filtered - jnp.mean(filtered, axis=1, keepdims=True)
    variance = jnp.mean(centered * centered, axis=1, keepdims=True)
    inverse = 1.0 / jnp.sqrt(variance + EPSILON)
    whitened = centered * inverse
    normed = whitened * norm_gain + norm_shift
    logistic = jax.nn.sigmoid(normed)
    activated = (normed * logistic).astype(jnp.bfloat16)
    shard_rows = weight.shape[0]
    every_act = lax.all_gather(activated, "fsdp", axis=0, tiled=True)
    cot_columns = lax.all_to_all(cotangent, "fsdp", split_axis=1, concat_axis=0, tiled=True)
    weight_shard = jnp.zeros((shard_rows, channels), jnp.float32)
    for source in range(fsdp_size):
        source_cot = cot_columns[source * row_count : (source + 1) * row_count]
        source_act = every_act[source * row_count : (source + 1) * row_count]
        term = lax.dot_general(
            source_cot, source_act, (((0,), (0,)), ((), ())), preferred_element_type=jnp.float32
        )
        weight_shard = weight_shard + term.astype(jnp.bfloat16).astype(jnp.float32)
    grad_normed = grad_hidden * logistic * (1.0 + normed * (1.0 - logistic))
    scaled = grad_normed * norm_gain
    grad_filtered = inverse * (
        scaled
        - jnp.mean(scaled, axis=1, keepdims=True)
        - whitened * jnp.mean(scaled * whitened, axis=1, keepdims=True)
    )
    grad_padded = jnp.pad(grad_filtered, ((half_taps, half_taps), (0, 0)))
    kernel_rows = []
    grad_owned = jnp.zeros_like(signal)
    for offset in range(tap_count):
        inside = (segment_pad[offset : offset + row_count] == segment).astype(jnp.float32)[:, None]
        kernel_rows.append(
            jnp.sum(grad_filtered * signal_pad[offset : offset + row_count] * inside, axis=0)
        )
        mirror = 2 * half_taps - offset
        mirrored = (segment_pad[mirror : mirror + row_count] == segment).astype(jnp.float32)[
            :, None
        ]
        grad_owned = (
            grad_owned + kernel[offset] * grad_padded[mirror : mirror + row_count] * mirrored
        )
    grad_owned = grad_owned.astype(jnp.bfloat16)
    kernel_part = jnp.stack(kernel_rows)
    gain_part = jnp.sum(grad_normed * whitened, axis=0)
    shift_part = jnp.sum(grad_normed, axis=0)
    owned_blocks = grad_owned.reshape(block_count, block_rows, channels)
    safe_slot = jnp.where(flat_slot < 0, 0, flat_slot)
    backward = jnp.where(
        (flat_slot >= 0)[:, None, None], owned_blocks[safe_slot], jnp.zeros((), jnp.bfloat16)
    )
    backward = backward.reshape(dp_size, capacity, block_rows, channels)
    returned = lax.all_to_all(backward, "dp", split_axis=0, concat_axis=0, tiled=True)
    grad_input = returned.reshape(dp_size * capacity, block_rows, channels)[send_place].reshape(
        row_count, channels
    )
    weight_total = lax.psum(weight_shard, "dp")
    kernel_total, gain_total, shift_total = lax.psum(
        (kernel_part, gain_part, shift_part), ("dp", "fsdp")
    )
    norm_scale = 1.0 / math.sqrt(row_count * dp_size * fsdp_size)
    return (
        grad_input,
        weight_total * norm_scale,
        kernel_total * norm_scale,
        gain_total * norm_scale,
        shift_total * norm_scale,
    )


def solution(mesh):
    placed = (
        P(("dp", "fsdp"), None),
        P(("dp", "fsdp")),
        P(("dp", "fsdp"), None),
        P(("dp", "fsdp"), None),
        P("fsdp", None),
        P(),
        P(),
        P(),
    )
    return jax.shard_map(
        on_device,
        mesh=mesh,
        in_specs=placed,
        out_specs=(P(("dp", "fsdp"), None), P("fsdp", None), P(), P(), P()),
        check_vma=False,
    )
```

profile of v0, /device:TPU:1, one launch (start us, length us, event | category | flops | bytes accessed | tf_op | source)
XLA Modules:
  0.0 652.3 jit_solution(2075874829294557923)
XLA Ops:
  10.3 11.6 %all-to-all-start = ((s32[64,1,1]{2,1,0:T(1,128)}), s32[64,1,1]{2,1,0:T(1,128)S(1)}, u32[]{:S(2)}, u32[]{:S(2)}) async-start(s32[64,1,1]{2,1,0:T(1,128)} %copy.18), calls=%async_computation | async-start | bytes 65536 | tf_op jit(solution)/shard_map/all_to_all | solution.py:49
  21.9 1.7 reshape.221
  24.7 8.1 %scatter_fusion = bf16[64,4,1536]{2,1,0:T(4,128)(2,1)} fusion(bf16[64,4,1536]{2,1,0:T(4,128)(2,1)} %broadcast_in_dim.26, s32[64]{0:T(128)S(1)} %compare_select_fusion.4, bf16[64,4,1536]{2,1,0:T(4,128)(2,1)S(1)} %reshape.221), kind=kCustom, calls=%fused_computation.3 | custom fusion | bytes 2359552 | tf_op jit(solution)/shard_map/scatter | solution.py:38
  32.8 10.3 %all-to-all-start.1 = ((bf16[64,1,4,1536]{3,2,1,0:T(4,128)(2,1)}), bf16[64,1,4,1536]{3,2,1,0:T(4,128)(2,1)S(1)}, u32[]{:S(2)}, u32[]{:S(2)}) async-start(bf16[64,1,4,1536]{3,2,1,0:T(4,128)(2,1)} %bitcast.2), calls=%async_computation.1 | async-start | bytes 1572864 | tf_op jit(solution)/shard_map/all_to_all | solution.py:48
  44.3 1.2 reduce.2
  46.2 19.9 %all-to-all-done.1 = bf16[64,1,4,1536]{3,2,1,0:T(4,128)(2,1)S(1)} async-done(((bf16[64,1,4,1536]{3,2,1,0:T(4,128)(2,1)}), bf16[64,1,4,1536]{3,2,1,0:T(4,128)(2,1)S(1)}, u32[]{:S(2)}, u32[]{:S(2)}) %all-to-all-start.1) | async-done | bytes 786464 | tf_op jit(solution)/shard_map/all_to_all | solution.py:48
  66.3 2.5 scatter_fusion.1
  69.5 12.6 %fusion.121 = (f32[256]{0:T(256)S(1)}, f32[256,1536]{1,0:T(8,128)S(1)}) fusion(f32[256]{0:T(256)S(1)} %get-tuple-element.106, f32[1536]{0:T(1024)S(1)} %get-tuple-element.69, f32[256]{0:T(256)S(1)} %get-tuple-element.78, f32[1536]{0:T(1024)S(1)} %get-tuple-element.70, f32[256]{0:T(256)S(1)} %get-tuple-element.79, f32[1536]{0:T(1024)S(1)} %get-tuple-element.41, ...), kind=kLoop, calls=%fused_computation.362 | loop fusion | flops 36175616 | bytes 3367936 | tf_op jit(solution)/shard_map/reduce_sum | solution.py:71
  83.5 6.6 %multiply_reduce_fusion = (f32[1536]{0:T(1024)}, f32[256]{0:T(256)}, f32[256]{0:T(256)}, f32[1536]{0:T(1024)}, bf16[256,1536]{1,0:T(8,128)(2,1)}, /*index=5*/f32[256,1536]{1,0:T(8,128)}) fusion(f32[256,1536]{1,0:T(8,128)S(1)} %get-tuple-element.75, f32[256]{0:T(256)} %add_rsqrt_fusion, f32[256]{0:T(256)} %copy-done.2, f32[1536]{0:T(1024)} %param.14, ...), kind=kOutput, calls=%fused_computation.182 | convolution fusion | flops 1216213504 | bytes 9465856 | tf_op jit(solution)/shard_map/dot_general | solution.py:56
  90.1 2.3 copy.19
  92.4 10.0 %all-to-all-start.3 = ((bf16[256,8,192]{0,2,1:T(8,128)(2,1)}), bf16[256,8,192]{0,2,1:T(8,128)(2,1)}, u32[]{:S(2)}, u32[]{:S(2)}) async-start(bf16[256,8,192]{0,2,1:T(8,128)(2,1)} %bitcast.46), calls=%async_computation.3 | async-start | bytes 1572864 | tf_op jit(solution)/shard_map/all_to_all | solution.py:80
  103.9 1.3 pad_clamp_fusion.1
  105.1 1.8 compare_reduce_fusion
  107.6 4.8 multiply_reduce_fusion.1
  112.4 3.2 multiply_reduce_fusion.10
  115.8 3.3 multiply_reduce_fusion.19
  119.2 1.4 multiply_reduce_fusion.28
  120.8 9.0 %fusion.93 = bf16[256,1536]{1,0:T(8,128)(2,1)S(1)} fusion(f32[256,1536]{1,0:T(8,128)S(1)} %get-tuple-element.73, f32[256]{0:T(256)S(1)} %get-tuple-element.106, f32[1536]{0:T(1024)S(1)} %get-tuple-element.69, f32[256]{0:T(256)S(1)} %get-tuple-element.78, f32[1536]{0:T(1024)S(1)} %get-tuple-element.70, f32[256]{0:T(256)S(1)} %get-tuple-element.79, ...), kind=kLoop, calls=%fused_computation.167 | loop fusion | flops 36175872 | bytes 2580480 | tf_op jit(solution)/shard_map/convert_element_type | solution.py:111
  130.0 2.8 stack.127
  132.8 1.3 gather_fusion
  134.2 100.4 %all-reduce.3 = (f32[1536]{0:T(1024)S(1)}, f32[1536]{0:T(1024)S(1)}) all-reduce(f32[1536]{0:T(1024)S(1)} %copy-done.3, f32[1536]{0:T(1024)S(1)} %copy-done.4), channel_id=1, replica_groups=mesh['dp'=64,'fsdp'=8] {'dp','fsdp'}, use_global_device_ids=true, to_apply=%region_44.45 | all-reduce | flops 3072 | bytes 24576 | tf_op jit(solution)/shard_map/psum | solution.py:126
  234.6 1.3 bitcast_select_fusion
  235.9 7.0 %all-to-all-start.2 = ((bf16[64,1,4,1536]{3,2,1,0:T(4,128)(2,1)}), bf16[64,1,4,1536]{3,2,1,0:T(4,128)(2,1)S(1)}, u32[]{:S(2)}, u32[]{:S(2)}) async-start(bf16[64,1,4,1536]{3,2,1,0:T(4,128)(2,1)} %bitcast_select_fusion), calls=%async_computation.2 | async-start | bytes 1572864 | tf_op jit(solution)/shard_map/all_to_all | solution.py:121
  243.2 1.5 fusion.16
  244.7 1.7 fusion.15
  246.4 1.9 fusion.13
  253.2 2.2 fusion.3
  256.1 193.1 %all-reduce.9.cloned.1.call-done = f32[31,1536]{1,0:T(8,128)} async-done(((f32[31,1536]{1,0:T(8,128)}), f32[31,1536]{1,0:T(8,128)}) %all-reduce.9.cloned.1.call-update) | async-done | bytes 190480 | tf_op jit(solution)/shard_map/psum | solution.py:126
  449.2 1.6 broadcast_multiply_fusion.1
  450.8 1.3 gather_fusion.1
  453.2 190.2 %all-reduce.7.cloned.1.call-done = f32[192,1536]{1,0:T(8,128)} async-done(((f32[192,1536]{1,0:T(8,128)}), f32[192,1536]{1,0:T(8,128)}) %all-reduce.7.cloned.1.call-update) | async-done | bytes 1179664 | tf_op jit(solution)/shard_map/psum | solution.py:125
  643.4 2.4 broadcast_multiply_fusion
  (88 shorter events, 17.6 us)
Async XLA Ops:
  7.2 76.3 %all-gather.3.cloned.1.call-start = ((), (), s32[]{:S(2)}) async-start(), calls=%async_computation.4 | async-start | bytes 5308416 | tf_op jit(solution)/shard_map/all_gather | solution.py:58
  8.8 24.0 %copy-start.6 = (s32[64]{0:T(128)}, s32[64]{0:T(128)S(1)}, u32[]{:S(2)}) copy-start(s32[64]{0:T(128)S(1)} %compare_select_fusion.4) | copy-start | bytes 772
  10.3 22.5 %all-to-all-start = ((s32[64,1,1]{2,1,0:T(1,128)}), s32[64,1,1]{2,1,0:T(1,128)S(1)}, u32[]{:S(2)}, u32[]{:S(2)}) async-start(s32[64,1,1]{2,1,0:T(1,128)} %copy.18), calls=%async_computation | async-start | bytes 65536 | tf_op jit(solution)/shard_map/all_to_all | solution.py:49
  24.7 18.7 %copy-start.7 = (s32[1,4]{1,0:T(1,128)S(1)}, s32[1,4]{1,0:T(1,128)}, u32[]{:S(2)}) copy-start(s32[1,4]{1,0:T(1,128)} %param.10) | copy-start | bytes 52
  24.7 19.0 %copy-start.1 = (f32[31,1536]{1,0:T(8,128)S(1)}, f32[31,1536]{1,0:T(8,128)}, u32[]{:S(2)}) copy-start(f32[31,1536]{1,0:T(8,128)} %param.13) | copy-start | bytes 571396
  32.8 33.3 %all-to-all-start.1 = ((bf16[64,1,4,1536]{3,2,1,0:T(4,128)(2,1)}), bf16[64,1,4,1536]{3,2,1,0:T(4,128)(2,1)S(1)}, u32[]{:S(2)}, u32[]{:S(2)}) async-start(bf16[64,1,4,1536]{3,2,1,0:T(4,128)(2,1)} %bitcast.2), calls=%async_computation.1 | async-start | bytes 1572864 | tf_op jit(solution)/shard_map/all_to_all | solution.py:48
  43.1 200.1 %all-gather.5.cloned.1.call-start = ((), (), s32[]{:S(2)}) async-start(), calls=%async_computation.5 | async-start | bytes 7077888 | tf_op jit(solution)/shard_map/all_gather | solution.py:79
  82.1 0.5 copy-start.2
  92.4 143.5 %all-to-all-start.3 = ((bf16[256,8,192]{0,2,1:T(8,128)(2,1)}), bf16[256,8,192]{0,2,1:T(8,128)(2,1)}, u32[]{:S(2)}, u32[]{:S(2)}) async-start(bf16[256,8,192]{0,2,1:T(8,128)(2,1)} %bitcast.46), calls=%async_computation.3 | async-start | bytes 1572864 | tf_op jit(solution)/shard_map/all_to_all | solution.py:80
  102.4 346.8 %all-reduce.9.cloned.1.call-start = ((), (), s32[]{:S(2)}) async-start(), calls=%async_computation.7 | async-start | bytes 393216 | tf_op jit(solution)/shard_map/psum | solution.py:126
  129.8 4.4 copy-start.3
  129.8 4.4 copy-start.4
  129.8 104.8 %copy-start.5 = (pred[64]{0:T(512)(128)(4,1)S(1)}, pred[64]{0:T(512)(128)(4,1)}, u32[]{:S(2)}) copy-start(pred[64]{0:T(512)(128)(4,1)} %compare_reduce_fusion) | copy-start | bytes 196
  235.9 214.9 %all-to-all-start.2 = ((bf16[64,1,4,1536]{3,2,1,0:T(4,128)(2,1)}), bf16[64,1,4,1536]{3,2,1,0:T(4,128)(2,1)S(1)}, u32[]{:S(2)}, u32[]{:S(2)}) async-start(bf16[64,1,4,1536]{3,2,1,0:T(4,128)(2,1)} %bitcast_select_fusion), calls=%async_computation.2 | async-start | bytes 1572864 | tf_op jit(solution)/shard_map/all_to_all | solution.py:121
  242.9 400.5 %all-reduce.7.cloned.1.call-start = ((), (), s32[]{:S(2)}) async-start(), calls=%async_computation.6 | async-start | bytes 2359296 | tf_op jit(solution)/shard_map/psum | solution.py:125
  244.7 3.6 copy-start
Sparse Core Ops, SparseCore 0:
  10.1 68.6 all-gather.2
  90.2 93.8 all-gather.4
  189.7 259.4 all-reduce.8
  453.4 189.9 all-reduce.6
where the time goes:
time: 655 us; the launch traced here: 652 us
  waiting for transfers between devices  404 us (62%)
  blocking collectives  100 us (15%)
  other arithmetic  49.2 us (8%)
  starting transfers between devices  39.8 us (6%)
  local copies, waits for them, and re-layouts  25.8 us (4%)
  matrix products  18.7 us (3%)
  between operations  14.3 us (2%)
    psum x1, waiting for transfers between devices, on_device(): lax.psum((kernel_part, gain_part, shift_part), ('dp', 'fsdp'))  193 us
    psum x1, waiting for transfers between devices, on_device(): weight_total = lax.psum(weight_shard, 'dp')  190 us
    psum x1, blocking collectives, on_device(): lax.psum((kernel_part, gain_part, shift_part), ('dp', 'fsdp'))  100 us
    all_to_all x1, waiting for transfers between devices, on_device(): lax.all_to_all(outgoing, 'dp', split_axis=0, concat_axis=0, tiled=True)  19.9 us
  transfers between devices with their start and end apart: 8, of which 3 were waited for; matrix products, arithmetic and copies ran while one was open for 13% of the time, Pallas kernels for 0%

commit v1 on v0

v1 whole, which is shorter than its diff:
```python
import functools
import math

import jax
import jax.numpy as jnp
from jax import lax
from jax.experimental import pallas as pl
from jax.experimental.pallas import tpu as pltpu
from jax.sharding import PartitionSpec as P

EPSILON = 1e-05
MESH = pl.DeviceIdType.MESH
F32 = jnp.float32
BF16 = jnp.bfloat16
BLOCK = 4
TAPS = 31
HALO = 16
KROWS = 40
VMEM_BYTES = 56 * 1024 * 1024


class Sizes:
    def __init__(self, dp_size, fsdp_size, rows, channels, shard):
        self.nd = dp_size
        self.nz = fsdp_size
        self.rows = rows
        self.ch = channels
        self.shard = shard
        self.nb = rows // BLOCK
        self.tiles = channels // 128
        self.groups = self.tiles // 4
        self.slab = 4 * self.tiles
        self.chips = dp_size // 2
        self.half = channels // 2
        self.ltiles = self.half // 128
        self.quarter = self.half // 2
        self.cuts = 4 if self.chips >= 4 * self.ltiles else 2
        self.prow = shard // self.cuts
        self.pieces = self.cuts * self.ltiles
        self.used = rows + 4 * HALO
        self.padded = self.used + 2 * HALO
        self.span = 80 if self.used % 80 == 0 else 48
        self.krow = 8 * (-(-(5 * self.ltiles) // self.chips))
        self.kall = self.krow * self.chips


def one_hot(mask):
    return jnp.where(mask, 1.0, 0.0).astype(BF16)


def dot(a, b):
    return jnp.dot(a, b, preferred_element_type=F32)


def greet(n, dp, z, steps):
    barrier = pltpu.get_barrier_semaphore()

    def along_dp(step, carry):
        pl.semaphore_signal(
            barrier, inc=1, device_id=(lax.rem(dp + step, n.nd), z), device_id_type=MESH
        )
        return carry

    lax.fori_loop(1, n.nd, along_dp, 0)
    for step in steps:
        pl.semaphore_signal(
            barrier, inc=1, device_id=(dp, lax.rem(z + step, n.nz)), device_id_type=MESH
        )
    pl.semaphore_wait(barrier, n.nd - 1 + len(steps))


def remote(src, dst, send, recv, dp, z):
    return pltpu.make_async_remote_copy(
        src_ref=src, dst_ref=dst, send_sem=send, recv_sem=recv, device_id=(dp, z), device_id_type=MESH
    )


def exchange_start(n, dp, z, src, dst, send, recv):
    def step_to(step, carry):
        peer = lax.rem(dp + step, n.nd)
        remote(src.at[peer], dst.at[dp], send.at[peer], recv.at[dp], peer, z).start()
        return carry

    lax.fori_loop(1, n.nd, step_to, 0)


def exchange_arrive(n, dp, z, src, dst, send, recv):
    def step_to(step, carry):
        peer = lax.rem(dp + step, n.nd)
        remote(src.at[peer], dst.at[peer], send.at[peer], recv.at[peer], peer, z).wait_recv()
        return carry

    lax.fori_loop(1, n.nd, step_to, 0)


def exchange_sent(n, dp, z, src, dst, send, recv):
    def step_to(step, carry):
        peer = lax.rem(dp + step, n.nd)
        remote(src.at[peer], dst.at[dp], send.at[peer], recv.at[dp], peer, z).wait_send()
        return carry

    lax.fori_loop(1, n.nd, step_to, 0)


def dispatch_kernel(
    n, code_ref, slots_ref, frames_ref, weight_ref,
    arrived_ref, label_ref, whole_ref,
    outgoing, b_send, b_recv, l_send, l_recv, u_send, u_recv, d_send, d_recv, s_send, s_recv,
):
    dp = lax.axis_index("dp")
    z = lax.axis_index("fsdp")
    core = lax.rem(dp, 2)
    mate = dp + 1 - 2 * core
    far = n.nz // 2
    up = lax.rem(z + 1, n.nz)
    down = lax.rem(z + n.nz - 1, n.nz)
    hrow = n.shard // 2
    steps = sorted({1, n.nz - 1})

    whole_ref[z] = weight_ref[...]
    code = code_ref[...]
    mats = []
    for jj in range(4):
        mats.append(
            jnp.concatenate(
                [frames_ref[:, 128 * (4 * g + jj) : 128 * (4 * g + jj + 1)] for g in range(n.groups)], axis=1
            )
        )
    chunk_rows = min(256, 16 * n.nb)

    def sort_chunk(chunk, carry):
        place = lax.broadcasted_iota(jnp.int32, (chunk_rows, n.rows), 0) + chunk * chunk_rows
        total = dot(one_hot(place == code), mats[0])
        for jj in range(1, 4):
            total = total + dot(one_hot(place == code + 4 * jj), mats[jj])
        for g in range(n.groups):
            part = total[:, 128 * g : 128 * (g + 1)].astype(BF16).reshape(chunk_rows // 16, 16, 128)
            outgoing[pl.ds(chunk * (chunk_rows // 16), chunk_rows // 16), 16 * g : 16 * (g + 1), :] = part
        return carry

    lax.fori_loop(0, 16 * n.nb // chunk_rows, sort_chunk, 0)
    arrived_ref[dp] = outgoing[dp]
    label_ref[dp] = slots_ref[dp]

    greet(n, dp, z, steps)

    def ring(step, block, first, count, to, send, recv):
        rows = pl.ds(pl.multiple_of(core * hrow + first, 16), count)
        return remote(
            whole_ref.at[block, rows], whole_ref.at[block, rows], send.at[step], recv.at[step], dp, to
        )

    def up_hop(step, block):
        last = step == far - 1
        return ring(step, block, 0, hrow // 2 if last else hrow, up, u_send, u_recv)

    def down_hop(step, block):
        last = step == far - 1
        return ring(step, block, hrow // 2 if last else 0, hrow // 2 if last else hrow, down, d_send, d_recv)

    def to_mate(slot, block):
        rows = pl.ds(pl.multiple_of(core * hrow, 16), hrow)
        return remote(
            whole_ref.at[block, rows], whole_ref.at[block, rows], s_send.at[slot], s_recv.at[slot], mate, z
        )

    up_hop(0, z).start()
    down_hop(0, z).start()
    exchange_start(n, dp, z, slots_ref, label_ref, l_send, l_recv)
    exchange_start(n, dp, z, outgoing, arrived_ref, b_send, b_recv)
    for step in range(far):
        below = lax.rem(z + n.nz - step - 1, n.nz)
        above = lax.rem(z + step + 1, n.nz)
        up_hop(step, below).wait_recv()
        if step < far - 1:
            up_hop(step + 1, below).start()
            to_mate(2 * step, below).start()
        down_hop(step, above).wait_recv()
        if step < far - 1:
            down_hop(step + 1, above).start()
            to_mate(2 * step + 1, above).start()
        else:
            to_mate(2 * step, above).start()
    exchange_arrive(n, dp, z, slots_ref, label_ref, l_send, l_recv)
    exchange_arrive(n, dp, z, outgoing, arrived_ref, b_send, b_recv)

    def from_mate(slot, block):
        rows = pl.ds(pl.multiple_of((1 - core) * hrow, 16), hrow)
        return remote(
            whole_ref.at[block, rows], whole_ref.at[block, rows], s_send.at[slot], s_recv.at[slot], mate, z
        )

    for step in range(far):
        below = lax.rem(z + n.nz - step - 1, n.nz)
        above = lax.rem(z + step + 1, n.nz)
        if step < far - 1:
            from_mate(2 * step, below).wait_recv()
            from_mate(2 * step + 1, above).wait_recv()
        else:
            from_mate(2 * step, above).wait_recv()
    for step in range(far):
        below = lax.rem(z + n.nz - step - 1, n.nz)
        above = lax.rem(z + step + 1, n.nz)
        up_hop(step, lax.rem(z + n.nz - step, n.nz)).wait_send()
        down_hop(step, lax.rem(z + step, n.nz)).wait_send()
        if step < far - 1:
            to_mate(2 * step, below).wait_send()
            to_mate(2 * step + 1, above).wait_send()
        else:
            to_mate(2 * step, above).wait_send()
    exchange_sent(n, dp, z, slots_ref, label_ref, l_send, l_recv)
    exchange_sent(n, dp, z, outgoing, arrived_ref, b_send, b_recv)


def dispatch(n, code_row, slots, frames, weight):
    far = n.nz // 2
    dma = pltpu.SemaphoreType.DMA
    return pl.pallas_call(
        functools.partial(dispatch_kernel, n),
        out_shape=(
            jax.ShapeDtypeStruct((n.nb, n.slab, 128), BF16),
            jax.ShapeDtypeStruct((n.nb, 1, 128), F32),
            jax.ShapeDtypeStruct((n.nz, n.shard, n.ch), BF16),
        ),
        in_specs=[pl.BlockSpec(memory_space=pltpu.VMEM)] * 4,
        out_specs=tuple([pl.BlockSpec(memory_space=pltpu.VMEM)] * 3),
        scratch_shapes=[
            pltpu.VMEM((n.nb, n.slab, 128), BF16),
            dma((n.nd,)), dma((n.nd,)), dma((n.nd,)), dma((n.nd,)),
            dma((far,)), dma((far,)), dma((far,)), dma((far,)),
            dma((2 * far,)), dma((2 * far,)),
        ],
        compiler_params=pltpu.CompilerParams(
            collective_id=0, has_side_effects=True, vmem_limit_bytes=VMEM_BYTES
        ),
    )(code_row, slots, frames, weight)


def padded_place(frame, ends):
    place = frame + HALO
    for end in ends:
        place = place + jnp.where(frame >= end, HALO, 0)
    return place


def compute_kernel(
    n, utt_ref, arrived_ref, label_ref, whole_ref, cot_ref, kernel_ref, gain_ref, shift_ref,
    back_ref, act_ref, kgrad_ref,
    xs, filt, hidden, gf, actp, go, labels, k8,
):
    ends = [utt_ref[0, 0]]
    for i in range(1, 3):
        ends.append(ends[-1] + utt_ref[0, i])
    lanes = 16 * n.nb

    lane = lax.broadcasted_iota(jnp.int32, (1, 128), 1)
    chunks = []
    for q in range(n.nb // 8):
        row = jnp.zeros((1, 128), F32)
        for s in range(8):
            row = row + jnp.where(lane // 16 == s, label_ref[8 * q + s], 0.0)
        chunks.append(row)
    slot_row = jnp.concatenate(chunks, axis=1).astype(jnp.int32)
    lane_all = lax.broadcasted_iota(jnp.int32, (1, lanes), 1)
    place_row = padded_place(slot_row * BLOCK + lane_all % 4, ends)

    def spread(src, carry):
        labels[pl.ds(pl.multiple_of(16 * src, 16), 16), :] = jnp.broadcast_to(label_ref[src], (16, 128))
        return carry

    lax.fori_loop(0, n.nb, spread, 0)

    blocks = jnp.concatenate(
        [arrived_ref[:, 16 * g : 16 * (g + 1), :].reshape(lanes, 128) for g in range(n.groups)], axis=1
    )
    row_iota = lax.broadcasted_iota(jnp.int32, (n.padded, lanes), 0)

    def put(jj, carry):
        mine = jnp.where((lane_all // 4) % 4 == jj, place_row, -1)
        owned = dot(one_hot(row_iota == mine), blocks)
        for g in range(n.groups):
            xs[4 * g + jj] = owned[:, 128 * g : 128 * (g + 1)]
        return carry

    lax.fori_loop(0, 4, put, 0)

    frame_row = padded_place(lax.broadcasted_iota(jnp.int32, (1, n.rows), 1), ends)
    pad_mat = one_hot(lax.broadcasted_iota(jnp.int32, (n.padded, n.rows), 0) == frame_row)
    cot_pad = dot(pad_mat, cot_ref[...]).astype(BF16)
    width = 512
    per = width // 128

    def project(i, carry):
        cols = pl.ds(pl.multiple_of(i * width, width), width)
        part = dot(cot_pad, whole_ref[:, :, cols].reshape(n.ch, width))
        for q in range(per):
            hidden[per * i + q] = part[:, 128 * q : 128 * (q + 1)]
        return carry

    lax.fori_loop(0, n.ch // width, project, 0)

    spans = range(n.used // n.span)

    def filter_tile(j, carry):
        taps = kernel_ref[j]
        for b in spans:
            base = 1 + n.span * b
            total = jnp.zeros((n.span, 128), F32)
            for s in range(8):
                window = xs[j, base + s : base + s + n.span + 24, :]
                for m in range(4):
                    k = s + 8 * m
                    if k < TAPS:
                        total = total + taps[k : k + 1] * window[8 * m : 8 * m + n.span]
            filt[j, HALO + n.span * b : HALO + n.span * (b + 1), :] = total
        return carry

    lax.fori_loop(0, n.tiles, filter_tile, 0)

    kgrad_ref[...] = jnp.zeros_like(kgrad_ref)
    actp[...] = jnp.zeros_like(actp)
    gf[:, :HALO, :] = jnp.zeros((n.tiles, HALO, 128), F32)
    gf[:, n.padded - HALO :, :] = jnp.zeros((n.tiles, HALO, 128), F32)

    def norm_span(b, carry):
        rows = pl.ds(pl.multiple_of(HALO + n.span * b, 16), n.span)
        total = filt[0, rows, :]
        for j in range(1, n.tiles):
            total = total + filt[j, rows, :]
        mean = jnp.sum(total, axis=1, keepdims=True) * (1.0 / n.ch)
        square = jnp.zeros((n.span, 128), F32)
        for j in range(n.tiles):
            centred = filt[j, rows, :] - mean
            square = square + centred * centred
        variance = jnp.sum(square, axis=1, keepdims=True) * (1.0 / n.ch)
        inverse = 1.0 / jnp.sqrt(variance + EPSILON)
        first = jnp.zeros((n.span, 128), F32)
        second = jnp.zeros((n.span, 128), F32)
        for j in range(n.tiles):
            gain = gain_ref[j]
            whitened = (filt[j, rows, :] - mean) * inverse
            normed = whitened * gain + shift_ref[j]
            logistic = 1.0 / (1.0 + jnp.exp(-normed))
            actp[rows, 128 * j : 128 * (j + 1)] = (normed * logistic).astype(BF16)
            grad_normed = hidden[j, rows, :] * logistic * (1.0 + normed * (1.0 - logistic))
            scaled = grad_normed * gain
            filt[j, rows, :] = whitened
            hidden[j, rows, :] = scaled
            first = first + scaled
            second = second + scaled * whitened
            half, at = j // n.ltiles, (j % n.ltiles) * KROWS
            kgrad_ref[half, at + TAPS : at + TAPS + 1, :] += jnp.sum(grad_normed * whitened, axis=0, keepdims=True)
            kgrad_ref[half, at + TAPS + 1 : at + TAPS + 2, :] += jnp.sum(grad_normed, axis=0, keepdims=True)
        mean1 = jnp.sum(first, axis=1, keepdims=True) * (1.0 / n.ch)
        mean2 = jnp.sum(second, axis=1, keepdims=True) * (1.0 / n.ch)
        for j in range(n.tiles):
            gf[j, rows, :] = inverse * (hidden[j, rows, :] - mean1 - filt[j, rows, :] * mean2)
        return carry

    lax.fori_loop(0, n.used // n.span, norm_span, 0)

    frame_col = padded_place(lax.broadcasted_iota(jnp.int32, (n.rows, 1), 0), ends)
    take = one_hot(lax.broadcasted_iota(jnp.int32, (n.rows, n.padded), 1) == frame_col)
    act_ref[...] = dot(take, actp[...]).astype(BF16)

    go[...] = jnp.zeros_like(go)

    def back_tile(j, carry):
        taps = kernel_ref[j]
        for b in spans:
            base = 1 + n.span * b
            here = slice(HALO + n.span * b, HALO + n.span * (b + 1))
            signal = xs[j, here, :]
            total = jnp.zeros((n.span, 128), F32)
            for s in range(8):
                window = gf[j, base + s : base + s + n.span + 24, :]
                for m in range(4):
                    k = TAPS - 1 - s - 8 * m
                    if k >= 0:
                        shifted = window[8 * m : 8 * m + n.span]
                        total = total + taps[k : k + 1] * shifted
                        product = jnp.sum((shifted * signal).reshape(n.span // 8, 8, 128), axis=0)
                        if b == 0:
                            k8[k] = product
                        else:
                            k8[k] += product
            go[j, here, :] = total.astype(BF16)
        at = pl.multiple_of(lax.rem(j, n.ltiles) * KROWS, 8)
        kgrad_ref[j // n.ltiles, pl.ds(at, TAPS), :] = jnp.sum(k8[...], axis=1)
        return carry

    lax.fori_loop(0, n.tiles, back_tile, 0)

    chunk_rows = min(256, lanes)

    def gather_chunk(chunk, carry):
        at = pl.ds(pl.multiple_of(chunk * chunk_rows, chunk_rows), chunk_rows)
        slot = labels[at, :][:, :1].astype(jnp.int32)
        sub = lax.broadcasted_iota(jnp.int32, (chunk_rows, 1), 0)
        place = padded_place(slot * BLOCK + sub % 4, ends)
        cols = lax.broadcasted_iota(jnp.int32, (chunk_rows, n.padded), 1)
        total = None
        for jj in range(4):
            mine = jnp.where((sub // 4) % 4 == jj, place, -1)
            rhs = jnp.concatenate([go[4 * g + jj] for g in range(n.groups)], axis=1)
            part = dot(one_hot(cols == mine), rhs)
            total = part if total is None else total + part
        for g in range(n.groups):
            part = total[:, 128 * g : 128 * (g + 1)].astype(BF16).reshape(chunk_rows // 16, 16, 128)
            back_ref[pl.ds(chunk * (chunk_rows // 16), chunk_rows // 16), 16 * g : 16 * (g + 1), :] = part
        return carry

    lax.fori_loop(0, lanes // chunk_rows, gather_chunk, 0)


def compute(n, lengths, arrived, labels, whole, cot, taps, gain, shift):
    vmem = pl.BlockSpec(memory_space=pltpu.VMEM)
    return pl.pallas_call(
        functools.partial(compute_kernel, n),
        out_shape=(
            jax.ShapeDtypeStruct((n.nb, n.slab, 128), BF16),
            jax.ShapeDtypeStruct((n.rows, n.ch), BF16),
            jax.ShapeDtypeStruct((2, n.kall, 128), F32),
        ),
        in_specs=[pl.BlockSpec(memory_space=pltpu.SMEM)] + [vmem] * 7,
        out_specs=(vmem,) * 3,
        scratch_shapes=[
            pltpu.VMEM((n.tiles, n.padded, 128), F32),
            pltpu.VMEM((n.tiles, n.padded, 128), F32),
            pltpu.VMEM((n.tiles, n.padded, 128), F32),
            pltpu.VMEM((n.tiles, n.padded, 128), F32),
            pltpu.VMEM((n.padded, n.ch), BF16),
            pltpu.VMEM((n.tiles, n.padded, 128), BF16),
            pltpu.VMEM((16 * n.nb, 128), F32),
            pltpu.VMEM((TAPS, 8, 128), F32),
        ],
        compiler_params=pltpu.CompilerParams(vmem_limit_bytes=VMEM_BYTES),
    )(lengths, arrived, labels, whole, cot, taps, gain, shift)


def finish_kernel(
    n, scale, code_ref, back_ref, act_ref, cot_ref, kgrad_ref,
    frames_out, weight_out, ksum_out,
    home, mate_act, mate_cot, mate_k, part, up_out, up_in, down_out, down_in,
    own_f, own_b, piece_in, all_b, mate_b, k_in, k_z, k_all, k_mate,
    h_send, h_recv, m_send, m_recv, u_send, u_recv, d_send, d_recv,
    p_send, p_recv, a_send, a_recv, ka_send, ka_recv, kz_send, kz_recv, kc_send, kc_recv,
):
    dp = lax.axis_index("dp")
    z = lax.axis_index("fsdp")
    core = lax.rem(dp, 2)
    mate = dp + 1 - 2 * core
    chip = dp // 2
    far = n.nz // 2
    up = lax.rem(z + 1, n.nz)
    down = lax.rem(z + n.nz - 1, n.nz)
    other = 1 - core
    mine = pl.ds(pl.multiple_of(core * n.half, 128), n.half)
    theirs = pl.ds(pl.multiple_of(other * n.half, 128), n.half)

    greet(n, dp, z, list(range(1, n.nz)))

    to_mate = [
        remote(kgrad_ref.at[other], mate_k, m_send.at[0], m_recv.at[0], mate, z),
        remote(cot_ref, mate_cot, m_send.at[1], m_recv.at[1], mate, z),
        remote(act_ref.at[:, theirs], mate_act, m_send.at[2], m_recv.at[2], mate, z),
    ]
    for copy in to_mate:
        copy.start()
    home[dp] = back_ref[dp]
    exchange_start(n, dp, z, back_ref, home, h_send, h_recv)

    def chips(body):
        lax.fori_loop(1, n.chips, lambda step, carry: (body(lax.rem(chip + step, n.chips)), carry)[1], 0)

    to_mate[0].wait_recv()
    mate_k[...] += kgrad_ref[core]

    def k_rows(at):
        return pl.ds(pl.multiple_of(at * n.krow, 8), n.krow)

    def k_scatter(at, slot):
        return remote(mate_k.at[k_rows(at)], k_in.at[slot], ka_send.at[at], ka_recv.at[slot], 2 * at + core, z)

    chips(lambda at: k_scatter(at, chip).start())

    to_mate[1].wait_recv()
    to_mate[2].wait_recv()
    width = 2 * n.shard
    turn = (((0,), (0,)), ((), ()))

    def product(i, carry):
        cols = pl.ds(pl.multiple_of(i * width, 128), width)
        total = lax.dot_general(cot_ref[:, cols], act_ref[:, mine], turn, preferred_element_type=F32)
        total = total + lax.dot_general(mate_cot[:, cols], mate_act[...], turn, preferred_element_type=F32)
        part[2 * i] = total[: n.shard]
        part[2 * i + 1] = total[n.shard :]
        return carry

    lax.fori_loop(0, n.nz // 2, product, 0)

    low, high = slice(0, n.quarter), slice(n.quarter, n.half)

    def up_hop(step):
        lanes = pl.ds(0, n.quarter if step == 0 else n.half)
        return remote(
            up_out.at[step, :, lanes], up_in.at[step, :, lanes], u_send.at[step], u_recv.at[step], dp, up
        )

    def down_hop(step):
        lanes = pl.ds(n.quarter, n.quarter) if step == 0 else pl.ds(0, n.half)
        return remote(
            down_out.at[step, :, lanes], down_in.at[step, :, lanes], d_send.at[step], d_recv.at[step], dp, down
        )

    across = lax.rem(z + far, n.nz)
    up_out[0, :, low] = part[across, :, low].astype(BF16)
    up_hop(0).start()
    down_out[0, :, high] = part[across, :, high].astype(BF16)
    down_hop(0).start()

    def k_sum(step, carry):
        return carry + k_in[lax.rem(chip + step, n.chips)]

    def k_over_z(slot, to):
        return remote(k_z.at[z], k_z.at[slot], kz_send.at[to], kz_recv.at[slot], dp, to)

    for step in range(1, far):
        target = lax.rem(z + far - step, n.nz)
        up_hop(step - 1).wait_recv()
        if step == 1:
            up_out[step, :, low] = (part[target, :, low] + up_in[0, :, low].astype(F32)).astype(BF16)
            up_out[step, :, high] = part[target, :, high].astype(BF16)
        else:
            up_out[step] = (part[target] + up_in[step - 1].astype(F32)).astype(BF16)
        up_hop(step).start()
        target = lax.rem(z + n.nz - far + step, n.nz)
        down_hop(step - 1).wait_recv()
        if step == 1:
            down_out[step, :, high] = (part[target, :, high] + down_in[0, :, high].astype(F32)).astype(BF16)
            down_out[step, :, low] = part[target, :, low].astype(BF16)
        else:
            down_out[step] = (part[target] + down_in[step - 1].astype(F32)).astype(BF16)
        down_hop(step).start()
        if step == 1:
            chips(lambda at: k_scatter(chip, at).wait_recv())
            k_in[chip] = mate_k[k_rows(chip), :]
            k_z[z] = lax.fori_loop(1, n.chips, k_sum, k_in[chip])
            for hop in range(1, n.nz):
                k_over_z(z, lax.rem(z + hop, n.nz)).start()

    for hop in range(1, n.nz):
        src = lax.rem(z + hop, n.nz)
        k_over_z(src, src).wait_recv()
    total = k_z[0]
    for i in range(1, n.nz):
        total = total + k_z[i]
    k_all[chip] = total * scale

    def k_gather(slot, to):
        return remote(k_all.at[slot], k_all.at[slot], kc_send.at[to], kc_recv.at[slot], 2 * to + core, z)

    chips(lambda at: k_gather(chip, at).start())

    up_hop(far - 1).wait_recv()
    down_hop(far - 1).wait_recv()
    if far == 1:
        part[z, :, low] += up_in[0, :, low].astype(F32)
        part[z, :, high] += down_in[0, :, high].astype(F32)
    else:
        part[z] += up_in[far - 1].astype(F32) + down_in[far - 1].astype(F32)

    for i in range(n.cuts):
        for l in range(n.ltiles):
            value = part[z, n.prow * i : n.prow * (i + 1), 128 * l : 128 * (l + 1)]
            own_f[i * n.ltiles + l] = value
            own_b[i * n.ltiles + l] = value.astype(BF16)

    def scatter(at, slot):
        return remote(own_b.at[at], piece_in.at[slot], p_send.at[at], p_recv.at[slot], 2 * at + core, z)

    def gather(slot, to):
        return remote(all_b.at[slot], all_b.at[slot], a_send.at[to], a_recv.at[slot], 2 * to + core, z)

    def scatter_start(at):
        @pl.when(at < n.pieces)
        def _():
            scatter(at, chip).start()

    chips(scatter_start)

    exchange_arrive(n, dp, z, back_ref, home, h_send, h_recv)
    code = code_ref[...]
    place = lax.broadcasted_iota(jnp.int32, (n.rows, 16 * n.nb), 1)
    blocks = jnp.concatenate(
        [home[:, 16 * g : 16 * (g + 1), :].reshape(16 * n.nb, 128) for g in range(n.groups)], axis=1
    )
    for jj in range(4):
        rows = dot(one_hot(place == code + 4 * jj), blocks).astype(BF16)
        for g in range(n.groups):
            frames_out[:, 128 * (4 * g + jj) : 128 * (4 * g + jj + 1)] = rows[:, 128 * g : 128 * (g + 1)]

    @pl.when(chip < n.pieces)
    def _():
        chips(lambda at: scatter(chip, at).wait_recv())
        total = lax.fori_loop(
            1, n.chips, lambda step, carry: carry + piece_in[lax.rem(chip + step, n.chips)].astype(F32), own_f[chip]
        )
        all_b[chip] = (total * scale).astype(BF16)
        chips(lambda at: gather(chip, at).start())

    def gather_arrive(at):
        @pl.when(at < n.pieces)
        def _():
            gather(at, at).wait_recv()

    chips(lambda at: k_gather(at, at).wait_recv())
    swap_k = remote(k_all, k_mate, m_send.at[3], m_recv.at[3], mate, z)
    swap_k.start()
    chips(gather_arrive)
    swap = remote(all_b, mate_b, m_send.at[4], m_recv.at[4], mate, z)
    swap.start()

    def lay(source, half):
        for i in range(n.cuts):
            for l in range(n.ltiles):
                cols = pl.ds(pl.multiple_of(half * n.half + 128 * l, 128), 128)
                weight_out[n.prow * i : n.prow * (i + 1), cols] = source[i * n.ltiles + l].astype(F32)

    lay(all_b, core)
    ksum_out[core] = k_all[...]
    swap_k.wait_recv()
    ksum_out[other] = k_mate[...]
    swap.wait_recv()
    lay(mate_b, other)

    swap.wait_send()
    swap_k.wait_send()
    for copy in to_mate:
        copy.wait_send()
    for step in range(far):
        up_hop(step).wait_send()
        down_hop(step).wait_send()
    for hop in range(1, n.nz):
        k_over_z(z, lax.rem(z + hop, n.nz)).wait_send()
    chips(lambda at: k_scatter(at, chip).wait_send())
    chips(lambda at: k_gather(chip, at).wait_send())

    def scatter_sent(at):
        @pl.when(at < n.pieces)
        def _():
            scatter(at, chip).wait_send()

    chips(scatter_sent)

    @pl.when(chip < n.pieces)
    def _():
        chips(lambda at: gather(chip, at).wait_send())

    exchange_sent(n, dp, z, back_ref, home, h_send, h_recv)


def finish(n, scale, code_col, back, act, cot, kgrad):
    far = n.nz // 2
    dma = pltpu.SemaphoreType.DMA
    vmem = pl.BlockSpec(memory_space=pltpu.VMEM)
    ring = pltpu.VMEM((far, n.shard, n.half), BF16)
    chips = dma((n.chips,))
    return pl.pallas_call(
        functools.partial(finish_kernel, n, scale),
        out_shape=(
            jax.ShapeDtypeStruct((n.rows, n.ch), BF16),
            jax.ShapeDtypeStruct((n.shard, n.ch), F32),
            jax.ShapeDtypeStruct((2, n.chips, n.krow, 128), F32),
        ),
        in_specs=[vmem] * 5,
        out_specs=(vmem,) * 3,
        scratch_shapes=[
            pltpu.VMEM((n.nb, n.slab, 128), BF16),
            pltpu.VMEM((n.rows, n.half), BF16),
            pltpu.VMEM((n.rows, n.ch), BF16),
            pltpu.VMEM((n.kall, 128), F32),
            pltpu.VMEM((n.nz, n.shard, n.half), F32),
            ring, ring, ring, ring,
            pltpu.VMEM((n.chips, n.prow, 128), F32),
            pltpu.VMEM((n.chips, n.prow, 128), BF16),
            pltpu.VMEM((n.chips, n.prow, 128), BF16),
            pltpu.VMEM((n.pieces, n.prow, 128), BF16),
            pltpu.VMEM((n.pieces, n.prow, 128), BF16),
            pltpu.VMEM((n.chips, n.krow, 128), F32),
            pltpu.VMEM((n.nz, n.krow, 128), F32),
            pltpu.VMEM((n.chips, n.krow, 128), F32),
            pltpu.VMEM((n.chips, n.krow, 128), F32),
            dma((n.nd,)), dma((n.nd,)),
            dma((5,)), dma((5,)),
            dma((far,)), dma((far,)), dma((far,)), dma((far,)),
            chips, chips, chips, chips, chips, chips,
            dma((n.nz,)), dma((n.nz,)),
            chips, chips,
        ],
        compiler_params=pltpu.CompilerParams(
            collective_id=1, has_side_effects=True, vmem_limit_bytes=VMEM_BYTES
        ),
    )(code_col, back, act, cot, kgrad)


def on_device(frames, destination, utt_lengths, cotangent, weight, kernel, norm_gain, norm_shift):
    n = Sizes(lax.axis_size("dp"), lax.axis_size("fsdp"), frames.shape[0], frames.shape[1], weight.shape[0])
    owner = destination // n.nb
    slot = destination % n.nb
    row = jnp.arange(n.rows, dtype=jnp.int32) % BLOCK
    code = jnp.repeat(owner, BLOCK) * 16 + row
    here = owner[None, :] == jnp.arange(n.nd, dtype=jnp.int32)[:, None]
    slots = jnp.sum(jnp.where(here, slot[None, :], 0), axis=1).astype(F32)
    slots = jnp.broadcast_to(slots[:, None, None], (n.nd, 1, 128))
    arrived, labels, whole = dispatch(n, code[None, :], slots, frames, weight)
    tiled = kernel.reshape(TAPS, n.tiles, 128).transpose(1, 0, 2)
    back, act, kgrad = compute(
        n, utt_lengths, arrived, labels, whole, cotangent, tiled,
        norm_gain.reshape(n.tiles, 1, 128), norm_shift.reshape(n.tiles, 1, 128),
    )
    scale = 1.0 / math.sqrt(n.rows * n.nd * n.nz)
    grad_input, grad_weight, ksum = finish(n, scale, code[:, None], back, act, cotangent, kgrad)
    ksum = ksum.reshape(2, n.kall, 128)[:, : KROWS * n.ltiles].reshape(n.tiles, KROWS, 128)
    ksum = ksum.transpose(1, 0, 2).reshape(KROWS, n.ch)
    return grad_input, grad_weight, ksum[:TAPS], ksum[TAPS], ksum[TAPS + 1]


def solution(mesh):
    placed = (
        P(("dp", "fsdp"), None),
        P(("dp", "fsdp")),
        P(("dp", "fsdp"), None),
        P(("dp", "fsdp"), None),
        P("fsdp", None),
        P(),
        P(),
        P(),
    )
    return jax.shard_map(
        on_device,
        mesh=mesh,
        in_specs=placed,
        out_specs=(P(("dp", "fsdp"), None), P("fsdp", None), P(), P(), P()),
        check_vma=False,
    )
```

time: 655 us -> 169 us (0.26)
  waiting for transfers between devices: 404 us -> 0 us
  Pallas kernels: 0 us -> 158 us
  blocking collectives: 100 us -> 0 us
  other arithmetic: 49.2 us -> 2.07 us
  starting transfers between devices: 39.8 us -> 0 us
  matrix products: 18.7 us -> 0 us
  local copies, waits for them, and re-layouts: 25.8 us -> 7.47 us
  between operations: 14.3 us -> 0.74 us
    psum x2 -> x0, waiting for transfers between devices: 383 us -> none  [the longest x1 193 us: on_device(): lax.psum((kernel_part, gain_part, shift_part), ('dp', 'fsdp'))]
    pallas_call x0 -> x3, Pallas kernels: none -> 158 us  [the longest x1 73.2 us: finish(): pl.pallas_call(functools.partial(finish_kernel, n, scale), out_shape=(jax...]
    psum x1 -> x0, blocking collectives: 100 us -> none  [on_device(): lax.psum((kernel_part, gain_part, shift_part), ('dp', 'fsdp'))]
    all_to_all x4 -> x0, starting transfers between devices: 39 us -> none  [the longest x1 11.6 us: on_device(): lax.all_to_all(labels, 'dp', split_axis=0, concat_axis=0, tiled=True)]
    reduce_sum x8 -> x1, other arithmetic: 25.8 us -> 0.11 us  [on_device(): slots = jnp.sum(jnp.where(here, slot[None, :], 0), axis=1).astype(F32)]
    all_to_all x4 -> x0, waiting for transfers between devices: 20 us -> none  [the longest x1 19.9 us: on_device(): lax.all_to_all(outgoing, 'dp', split_axis=0, concat_axis=0, tiled=True)]
    dot_general x9 -> x0, matrix products: 18.7 us -> none  [the longest x8 12.2 us: on_device(): lax.dot_general(source_cot, source_act, (((0,), (0,)), ((), ())), preferr...]
    scatter x3 -> x0, local copies, waits for them, and re-layouts: 11.4 us -> none  [the longest x1 8.1 us: on_device(): outgoing = jnp.zeros((dp_size * capacity, block_rows, channels), jnp.bflo...]
  transfers between devices with their start and end apart: 8 -> 0, of which waited for: 3 -> 0; matrix products, arithmetic and copies ran while one was open for 13% -> 0% of each run, Pallas kernels for 0% -> 0%
where the time goes in v1:
time: 169 us; the launch traced here: 168 us
  Pallas kernels  158 us (93%)
  local copies, waits for them, and re-layouts  7.47 us (4%)
  other arithmetic  2.07 us (1%)
    pallas_call x1, Pallas kernels, finish(): pl.pallas_call(functools.partial(finish_kernel, n, scale), out_shape=(jax...  73.2 us
    pallas_call x1, Pallas kernels, dispatch(): pl.pallas_call(functools.partial(dispatch_kernel, n), out_shape=(jax.Shap...  56.5 us
    pallas_call x1, Pallas kernels, compute(): pl.pallas_call(functools.partial(compute_kernel, n), out_shape=(jax.Shape...  28.1 us

profile of v1, /device:TPU:1, one launch (start us, length us, event | category | flops | bytes accessed | tf_op | source)
XLA Modules:
  0.0 168.2 jit_solution(10066048970076024820)
XLA Ops:
  0.6 0.0 copy-start.2
  0.6 0.7 broadcast_multiply_fusion
  1.3 0.1 select_reduce_fusion
  1.5 0.8 broadcast_in_dim.29.slots_ref
  2.2 0.1 broadcast_in_dim.16
  2.3 0.0 copy-start.3
  2.3 0.0 copy-start.4
  2.3 0.1 mul.31
  2.4 0.6 fusion.4.code_ref
  3.0 56.5 %shard_map.119 = (bf16[64,48,128]{2,1,0:T(8,128)(2,1)}, f32[64,1,128]{2,1,0:T(1,128)}, bf16[8,192,1536]{2,1,0:T(8,128)(2,1)}) custom-call(s32[1,256]{1,0:T(1,128)} %fusion.4.code_ref, f32[64,1,128]{2,1,0:T(1,128)} %broadcast_in_dim.29.slots_ref, bf16[256,1536]{1,0:T(8,128)(2,1)} %frames_ref.1, bf16[192,1536]{1,0:T(8,128)(2,1)} %weight_ref.1), custom_call_target="tpu_custom_call" | custom-call | tf_op jit(solution)/shard_map/pallas_call | solution.py:218
  59.5 0.0 copy-done.2
  59.6 0.7 copy.24
  60.3 0.0 copy-done.3
  60.3 0.6 reshape.114.gain_ref
  60.9 0.0 copy-done.4
  60.9 0.6 reshape.115.shift_ref
  61.5 28.1 %shard_map.120 = (bf16[64,48,128]{2,1,0:T(8,128)(2,1)}, bf16[256,1536]{1,0:T(8,128)(2,1)}, f32[2,256,128]{2,1,0:T(8,128)}) custom-call(s32[1,4]{1,0:T(1,128)} %utt_ref.1, bf16[64,48,128]{2,1,0:T(8,128)(2,1)} %get-tuple-element.14.arrived_ref, f32[64,1,128]{2,1,0:T(1,128)} %get-tuple-element.15.label_ref, bf16[8,192,1536]{2,1,0:T(8,128)(2,1)} %get-tuple-element.16.whole_ref, ...), custom_call_target="tpu_custom_call" | custom-call | tf_op jit(solution)/shard_map/pallas_call | solution.py:418
  89.7 0.1 mul.32
  89.8 0.7 fusion.code_ref
  90.4 73.2 %shard_map.121 = (bf16[256,1536]{1,0:T(8,128)(2,1)}, f32[192,1536]{1,0:T(8,128)}, f32[2,32,8,128]{3,2,1,0:T(8,128)}) custom-call(s32[256,1]{1,0:T(8,128)} %fusion.code_ref, bf16[64,48,128]{2,1,0:T(8,128)(2,1)} %get-tuple-element.17.back_ref, bf16[256,1536]{1,0:T(8,128)(2,1)} %get-tuple-element.18.act_ref, bf16[256,1536]{1,0:T(8,128)(2,1)} %cot_ref.3, ...), custom_call_target="tpu_custom_call" | custom-call | tf_op jit(solution)/shard_map/pallas_call | solution.py:669
  163.7 0.0 copy-start.1
  163.7 1.0 slice.22
  164.8 0.1 copy.21
  164.9 0.0 copy-start
  164.9 0.7 copy.22
  165.7 0.6 slice_reduce_fusion
  166.3 0.0 copy-done.1
  166.3 0.9 copy.27
  167.2 0.0 copy-done
  167.2 1.0 copy.28
  (4 shorter events, 0.1 us)
Async XLA Ops:
  0.6 58.9 %copy-start.2 = (f32[31,1536]{1,0:T(8,128)S(1)}, f32[31,1536]{1,0:T(8,128)}, u32[]{:S(2)}) copy-start(f32[31,1536]{1,0:T(8,128)} %param.13) | copy-start | bytes 571396
  2.3 58.0 %copy-start.3 = (f32[1536]{0:T(1024)S(1)}, f32[1536]{0:T(1024)}, u32[]{:S(2)}) copy-start(f32[1536]{0:T(1024)} %param.14) | copy-start | bytes 18436
  2.3 58.6 %copy-start.4 = (f32[1536]{0:T(1024)S(1)}, f32[1536]{0:T(1024)}, u32[]{:S(2)}) copy-start(f32[1536]{0:T(1024)} %param.15) | copy-start | bytes 18436
  163.7 2.6 %copy-start.1 = (bf16[256,1536]{1,0:T(8,128)(2,1)S(1)}, bf16[256,1536]{1,0:T(8,128)(2,1)}, u32[]{:S(2)}) copy-start(bf16[256,1536]{1,0:T(8,128)(2,1)} %get-tuple-element.33) | copy-start | bytes 2359300
  164.9 2.3 %copy-start = (f32[192,1536]{1,0:T(8,128)S(1)}, f32[192,1536]{1,0:T(8,128)}, u32[]{:S(2)}) copy-start(f32[192,1536]{1,0:T(8,128)} %get-tuple-element.34) | copy-start | bytes 3538948

commit v2 on v0

v2 whole, which is shorter than its diff:
```python
import functools
import math

import jax
import jax.numpy as jnp
from jax import lax
from jax.experimental import pallas as pl
from jax.experimental.pallas import tpu as pltpu
from jax.sharding import PartitionSpec as P

EPSILON = 1e-05
MESH = pl.DeviceIdType.MESH
F32 = jnp.float32
BF16 = jnp.bfloat16
BLOCK = 4
TAPS = 31
HALO = 16
KROWS = 40
VMEM_BYTES = 56 * 1024 * 1024


class Sizes:
    def __init__(self, dp_size, fsdp_size, rows, channels, shard):
        self.nd = dp_size
        self.nz = fsdp_size
        self.rows = rows
        self.ch = channels
        self.shard = shard
        self.nb = rows // BLOCK
        self.tiles = channels // 128
        self.groups = self.tiles // 4
        self.slab = 4 * self.tiles
        self.chips = dp_size // 2
        self.half = channels // 2
        self.ltiles = self.half // 128
        self.quarter = self.half // 2
        self.nx = 4 if self.chips >= 32 else 2
        self.ny = self.chips // self.nx
        self.prow = shard // self.nx
        self.used = rows + 4 * HALO
        self.padded = self.used + 2 * HALO
        self.span = 80 if self.used % 80 == 0 else 48
        self.krow = 8 * (-(-(5 * self.ltiles) // self.chips))
        self.kall = self.krow * self.chips


def one_hot(mask):
    return jnp.where(mask, 1.0, 0.0).astype(BF16)


def dot(a, b):
    return jnp.dot(a, b, preferred_element_type=F32)


def remote(src, dst, send, recv, dp, z):
    return pltpu.make_async_remote_copy(
        src_ref=src, dst_ref=dst, send_sem=send, recv_sem=recv, device_id=(dp, z), device_id_type=MESH
    )


def padded_place(frame, ends):
    place = frame + HALO
    for end in ends:
        place = place + jnp.where(frame >= end, HALO, 0)
    return place


def module_kernel(
    n, scale,
    dest_ref, utt_ref, frames_ref, cot_ref, weight_ref, taps_ref, gain_ref, shift_ref,
    frames_out, weight_out, taps_out, gain_out, shift_out,
    outgoing, arrived, label_out, label_in, labels, whole,
    xs, filt, hidden, gf, slope, spread, actp, go, k8, kgrad, cot_pad, cot_turned, mate_cot, act_both, act_send,
    part, up_out, up_in, down_out, down_in, back, home,
    x_out, x_in, y_own, y_out, y_in, y_all, x_all, x_mate, mate_k, k_in, k_z, k_all, k_mate,
    b_send, b_recv, l_send, l_recv, h_send, h_recv,
    gu_send, gu_recv, gd_send, gd_recv, gm_send, gm_recv, m_send, m_recv,
    u_send, u_recv, d_send, d_recv,
    xr_send, xr_recv, yr_send, yr_recv, yg_send, yg_recv, xg_send, xg_recv,
    ka_send, ka_recv, kz_send, kz_recv, kc_send, kc_recv,
):
    dp = lax.axis_index("dp")
    z = lax.axis_index("fsdp")
    core = lax.rem(dp, 2)
    other = 1 - core
    mate = dp + 1 - 2 * core
    chip = dp // 2
    cx = chip // n.ny
    cy = lax.rem(chip, n.ny)
    far = n.nz // 2
    up = lax.rem(z + 1, n.nz)
    down = lax.rem(z + n.nz - 1, n.nz)
    hrow = n.shard // 2
    lanes = 16 * n.nb
    spans = range(n.used // n.span)
    mine = pl.ds(pl.multiple_of(core * n.half, 128), n.half)
    theirs = pl.ds(pl.multiple_of(other * n.half, 128), n.half)

    barrier = pltpu.get_barrier_semaphore()

    def along_dp(step, carry):
        pl.semaphore_signal(
            barrier, inc=1, device_id=(lax.rem(dp + step, n.nd), z), device_id_type=MESH
        )
        return carry

    lax.fori_loop(1, n.nd, along_dp, 0)
    for step in range(1, n.nz):
        pl.semaphore_signal(
            barrier, inc=1, device_id=(dp, lax.rem(z + step, n.nz)), device_id_type=MESH
        )

    whole[z] = weight_ref[...]

    lane128 = lax.broadcasted_iota(jnp.int32, (1, 128), 1)
    lane_rows = lax.broadcasted_iota(jnp.int32, (1, n.rows), 1)

    def read_block(b, carry):
        code, owners, slots = carry
        dest = dest_ref[b]
        owner = dest // n.nb
        slot = dest - owner * n.nb
        code = jnp.where(lane_rows // BLOCK == b, owner * 16, code)
        owners = jnp.where(lane128 == b, owner, owners)
        slots = jnp.where(lane128 == b, slot, slots)
        return code, owners, slots

    start = (jnp.zeros((1, n.rows), jnp.int32), jnp.full((1, 128), -1, jnp.int32), jnp.zeros((1, 128), jnp.int32))
    code, owners, slots = lax.fori_loop(0, n.nb, read_block, start)
    code = code + lane_rows % BLOCK
    owner_iota = lax.broadcasted_iota(jnp.int32, (n.nd, 128), 0)
    slot_of = jnp.sum(jnp.where(owner_iota == owners, slots, 0).astype(F32), axis=1, keepdims=True)
    slot_of = jnp.broadcast_to(slot_of, (n.nd, 128))
    for i in range(n.nd):
        label_out[i] = slot_of[i : i + 1]

    mats = [
        jnp.concatenate(
            [frames_ref[:, 128 * (4 * g + jj) : 128 * (4 * g + jj + 1)] for g in range(n.groups)], axis=1
        )
        for jj in range(4)
    ]
    chunk_rows = min(256, lanes)
    per_chunk = chunk_rows // 16

    def sort_chunk(chunk, carry):
        place = lax.broadcasted_iota(jnp.int32, (chunk_rows, n.rows), 0) + chunk * chunk_rows
        total = dot(one_hot(place == code), mats[0])
        for jj in range(1, 4):
            total = total + dot(one_hot(place == code + 4 * jj), mats[jj])
        for g in range(n.groups):
            piece = total[:, 128 * g : 128 * (g + 1)].astype(BF16).reshape(per_chunk, 16, 128)
            outgoing[pl.ds(chunk * per_chunk, per_chunk), 16 * g : 16 * (g + 1), :] = piece
        return carry

    lax.fori_loop(0, lanes // chunk_rows, sort_chunk, 0)

    pl.semaphore_wait(barrier, n.nd - 1 + n.nz - 1)

    def gather_hop(step, block, first, count, to, send, recv):
        rows = pl.ds(pl.multiple_of(core * hrow + first, 16), count)
        return remote(whole.at[block, rows], whole.at[block, rows], send.at[step], recv.at[step], dp, to)

    def gather_up(step, block):
        last = step == far - 1
        return gather_hop(step, block, 0, hrow // 2 if last else hrow, up, gu_send, gu_recv)

    def gather_down(step, block):
        last = step == far - 1
        return gather_hop(step, block, hrow // 2 if last else 0, hrow // 2 if last else hrow, down, gd_send, gd_recv)

    def gather_mate(slot, block, half):
        rows = pl.ds(pl.multiple_of(half * hrow, 16), hrow)
        return remote(whole.at[block, rows], whole.at[block, rows], gm_send.at[slot], gm_recv.at[slot], mate, z)

    def below(step):
        return lax.rem(z + n.nz - step - 1, n.nz)

    def above(step):
        return lax.rem(z + step + 1, n.nz)

    def gather_pass(step):
        gather_up(step, below(step)).wait_recv()
        if step < far - 1:
            gather_up(step + 1, below(step)).start()
            gather_mate(2 * step, below(step), core).start()
        gather_down(step, above(step)).wait_recv()
        if step < far - 1:
            gather_down(step + 1, above(step)).start()
            gather_mate(2 * step + 1, above(step), core).start()
        else:
            gather_mate(2 * step, above(step), core).start()

    gather_up(0, z).start()
    gather_down(0, z).start()

    def block_to(peer):
        return remote(outgoing.at[peer], arrived.at[dp], b_send.at[peer], b_recv.at[dp], peer, z)

    def block_from(peer):
        return remote(outgoing.at[peer], arrived.at[peer], b_send.at[peer], b_recv.at[peer], peer, z)

    def label_to(peer):
        return remote(label_out.at[peer], label_in.at[dp], l_send.at[peer], l_recv.at[dp], peer, z)

    def label_from(peer):
        return remote(label_out.at[peer], label_in.at[peer], l_send.at[peer], l_recv.at[peer], peer, z)

    def peers(body):
        def step_to(step, carry):
            body(lax.rem(dp + step, n.nd))
            return carry

        lax.fori_loop(1, n.nd, step_to, 0)

    def chips(body):
        def step_to(step, carry):
            body(lax.rem(chip + step, n.chips))
            return carry

        lax.fori_loop(1, n.chips, step_to, 0)

    def send_block(peer):
        label_to(peer).start()
        block_to(peer).start()

    peers(send_block)
    swap_cot = remote(cot_ref, mate_cot, m_send.at[0], m_recv.at[0], mate, z)
    swap_cot.start()
    arrived[dp] = outgoing[dp]
    label_in[dp] = label_out[dp]

    ends = [utt_ref[0, 0]]
    for i in range(1, 3):
        ends.append(ends[-1] + utt_ref[0, i])
    frame_row = padded_place(lane_rows, ends)
    pad_mat = one_hot(lax.broadcasted_iota(jnp.int32, (n.padded, n.rows), 0) == frame_row)
    cot_pad[...] = dot(pad_mat, cot_ref[...]).astype(BF16)
    cot_turned[:, : n.rows] = cot_ref[...].T
    kgrad[...] = jnp.zeros_like(kgrad)
    actp[...] = jnp.zeros_like(actp)
    go[...] = jnp.zeros_like(go)
    gf[:, :HALO, :] = jnp.zeros((n.tiles, HALO, 128), F32)
    gf[:, n.padded - HALO :, :] = jnp.zeros((n.tiles, HALO, 128), F32)
    swap_cot.wait_recv()
    cot_turned[:, n.rows :] = mate_cot[...].T

    for step in range(far - 1):
        gather_pass(step)

    peers(lambda peer: label_from(peer).wait_recv())
    chunks = []
    for q in range(n.nb // 8):
        row = jnp.zeros((1, 128), F32)
        for s in range(8):
            row = row + jnp.where(lane128 // 16 == s, label_in[8 * q + s], 0.0)
        chunks.append(row)
    slot_row = jnp.concatenate(chunks, axis=1).astype(jnp.int32)
    lane_all = lax.broadcasted_iota(jnp.int32, (1, lanes), 1)
    place_row = padded_place(slot_row * BLOCK + lane_all % 4, ends)

    def lay_label(src, carry):
        labels[pl.ds(pl.multiple_of(16 * src, 16), 16), :] = jnp.broadcast_to(label_in[src], (16, 128))
        return carry

    lax.fori_loop(0, n.nb, lay_label, 0)

    peers(lambda peer: block_from(peer).wait_recv())
    blocks = jnp.concatenate(
        [arrived[:, 16 * g : 16 * (g + 1), :].reshape(lanes, 128) for g in range(n.groups)], axis=1
    )
    row_iota = lax.broadcasted_iota(jnp.int32, (n.padded, lanes), 0)

    def put(jj, carry):
        owned = dot(one_hot(row_iota == jnp.where((lane_all // 4) % 4 == jj, place_row, -1)), blocks)
        for g in range(n.groups):
            xs[4 * g + jj] = owned[:, 128 * g : 128 * (g + 1)]
        return carry

    lax.fori_loop(0, 4, put, 0)

    def filter_tile(j, carry):
        taps = taps_ref[:, pl.ds(pl.multiple_of(j * 128, 128), 128)]
        for b in spans:
            base = 1 + n.span * b
            total = jnp.zeros((n.span, 128), F32)
            for s in range(8):
                window = xs[j, base + s : base + s + n.span + 24, :]
                for m in range(4):
                    k = s + 8 * m
                    if k < TAPS:
                        total = total + taps[k : k + 1] * window[8 * m : 8 * m + n.span]
            filt[j, HALO + n.span * b : HALO + n.span * (b + 1), :] = total
        return carry

    lax.fori_loop(0, n.tiles, filter_tile, 0)

    def norm_span(b, carry):
        rows = pl.ds(pl.multiple_of(HALO + n.span * b, 16), n.span)
        total = filt[0, rows, :]
        for j in range(1, n.tiles):
            total = total + filt[j, rows, :]
        mean = jnp.sum(total, axis=1, keepdims=True) * (1.0 / n.ch)
        square = jnp.zeros((n.span, 128), F32)
        for j in range(n.tiles):
            centred = filt[j, rows, :] - mean
            square = square + centred * centred
        variance = jnp.sum(square, axis=1, keepdims=True) * (1.0 / n.ch)
        inverse = 1.0 / jnp.sqrt(variance + EPSILON)
        spread[rows, :] = jnp.broadcast_to(inverse, (n.span, 128))
        for j in range(n.tiles):
            whitened = (filt[j, rows, :] - mean) * inverse
            normed = whitened * gain_ref[:, 128 * j : 128 * (j + 1)] + shift_ref[:, 128 * j : 128 * (j + 1)]
            logistic = 1.0 / (1.0 + jnp.exp(-normed))
            activated = normed * logistic
            actp[rows, 128 * j : 128 * (j + 1)] = activated.astype(BF16)
            filt[j, rows, :] = whitened
            slope[j, rows, :] = logistic * (1.0 + normed * (1.0 - logistic))
        return carry

    lax.fori_loop(0, n.used // n.span, norm_span, 0)

    frame_col = padded_place(lax.broadcasted_iota(jnp.int32, (n.rows, 1), 0), ends)
    take = one_hot(lax.broadcasted_iota(jnp.int32, (n.rows, n.padded), 1) == frame_col)
    act_send[...] = dot(take, actp[:, theirs]).astype(BF16)
    swap_act = remote(act_send, act_both.at[pl.ds(n.rows, n.rows)], m_send.at[1], m_recv.at[1], mate, z)
    swap_act.start()
    act_both[: n.rows] = dot(take, actp[:, mine]).astype(BF16)

    gather_pass(far - 1)
    for step in range(far):
        gather_mate(2 * step, below(step) if step < far - 1 else above(step), other).wait_recv()
        if step < far - 1:
            gather_mate(2 * step + 1, above(step), other).wait_recv()
    width = 512
    per = width // 128

    def project(i, carry):
        cols = pl.ds(pl.multiple_of(i * width, width), width)
        piece = dot(cot_pad[...], whole[:, :, cols].reshape(n.ch, width))
        for q in range(per):
            hidden[per * i + q] = piece[:, 128 * q : 128 * (q + 1)]
        return carry

    lax.fori_loop(0, n.ch // width, project, 0)

    swap_act.wait_recv()

    def product(target):
        part[target] = dot(cot_turned[pl.ds(pl.multiple_of(target * n.shard, 16), n.shard), :], act_both[...])

    chunk_of = [slice(0, n.quarter), slice(n.quarter, n.half)]

    def ring_hop(way, chunk, step):
        out, into, send, recv, to = (
            (up_out, up_in, u_send, u_recv, up) if way == 0 else (down_out, down_in, d_send, d_recv, down)
        )
        at = far * chunk + step
        return remote(out.at[chunk, step], into.at[chunk, step], send.at[at], recv.at[at], dp, to)

    def ring_target(way, chunk, step):
        ahead = (far if way == chunk else far - 1) - step
        return lax.rem(z + ahead, n.nz) if way == 0 else lax.rem(z + n.nz - ahead, n.nz)

    def ring_steps(way, chunk):
        return far if way == chunk else far - 1

    def ring_step(step):
        for way, chunk in ((0, 0), (1, 1), (0, 1), (1, 0)):
            if step < ring_steps(way, chunk):
                out, into = (up_out, up_in) if way == 0 else (down_out, down_in)
                value = part[ring_target(way, chunk, step), :, chunk_of[chunk]]
                if step > 0:
                    ring_hop(way, chunk, step - 1).wait_recv()
                    value = value + into[chunk, step - 1].astype(F32)
                out[chunk, step] = value.astype(BF16)
                ring_hop(way, chunk, step).start()

    product(lax.rem(z + far, n.nz))
    if far > 1:
        product(lax.rem(z + far - 1, n.nz))
        product(lax.rem(z + n.nz - far + 1, n.nz))
    ring_step(0)

    def products(i, carry):
        product(lax.rem(z + n.nz - far + 2 + i, n.nz))
        return carry

    if far > 1:
        lax.fori_loop(0, n.nz - 3, products, 0)
    else:
        product(z)

    def norm_back(b, carry):
        rows = pl.ds(pl.multiple_of(HALO + n.span * b, 16), n.span)
        first = jnp.zeros((n.span, 128), F32)
        second = jnp.zeros((n.span, 128), F32)
        for j in range(n.tiles):
            whitened = filt[j, rows, :]
            grad_normed = hidden[j, rows, :] * slope[j, rows, :]
            scaled = grad_normed * gain_ref[:, 128 * j : 128 * (j + 1)]
            hidden[j, rows, :] = scaled
            first = first + scaled
            second = second + scaled * whitened
            half, at = j // n.ltiles, (j % n.ltiles) * KROWS
            kgrad[half, at + TAPS : at + TAPS + 1, :] += jnp.sum(grad_normed * whitened, axis=0, keepdims=True)
            kgrad[half, at + TAPS + 1 : at + TAPS + 2, :] += jnp.sum(grad_normed, axis=0, keepdims=True)
        mean1 = jnp.sum(first, axis=1, keepdims=True) * (1.0 / n.ch)
        mean2 = jnp.sum(second, axis=1, keepdims=True) * (1.0 / n.ch)
        inverse = spread[rows, :]
        for j in range(n.tiles):
            gf[j, rows, :] = inverse * (hidden[j, rows, :] - mean1 - filt[j, rows, :] * mean2)
        return carry

    lax.fori_loop(0, n.used // n.span, norm_back, 0)

    def back_tile(j, carry):
        taps = taps_ref[:, pl.ds(pl.multiple_of(j * 128, 128), 128)]
        for b in spans:
            base = 1 + n.span * b
            here = slice(HALO + n.span * b, HALO + n.span * (b + 1))
            signal = xs[j, here, :]
            total = jnp.zeros((n.span, 128), F32)
            for s in range(8):
                window = gf[j, base + s : base + s + n.span + 24, :]
                for m in range(4):
                    k = TAPS - 1 - s - 8 * m
                    if k >= 0:
                        shifted = window[8 * m : 8 * m + n.span]
                        total = total + taps[k : k + 1] * shifted
                        product = jnp.sum((shifted * signal).reshape(n.span // 8, 8, 128), axis=0)
                        if b == 0:
                            k8[k] = product
                        else:
                            k8[k] += product
            go[j, here, :] = total.astype(BF16)
        at = pl.multiple_of(lax.rem(j, n.ltiles) * KROWS, 8)
        kgrad[j // n.ltiles, pl.ds(at, TAPS), :] = jnp.sum(k8[...], axis=1)
        return carry

    third = n.tiles // 3
    lax.fori_loop(0, third, back_tile, 0)
    if far > 1:
        ring_step(1)
    lax.fori_loop(third, n.tiles, back_tile, 0)
    swap_k = remote(kgrad.at[other], mate_k, m_send.at[2], m_recv.at[2], mate, z)
    swap_k.start()
    if far > 2:
        ring_step(2)

    def gather_chunk(chunk, carry):
        at = pl.ds(pl.multiple_of(chunk * chunk_rows, chunk_rows), chunk_rows)
        slot = labels[at, :][:, :1].astype(jnp.int32)
        sub = lax.broadcasted_iota(jnp.int32, (chunk_rows, 1), 0)
        place = padded_place(slot * BLOCK + sub % 4, ends)
        cols = lax.broadcasted_iota(jnp.int32, (chunk_rows, n.padded), 1)
        total = None
        for jj in range(4):
            rhs = jnp.concatenate([go[4 * g + jj] for g in range(n.groups)], axis=1)
            piece = dot(one_hot(cols == jnp.where((sub // 4) % 4 == jj, place, -1)), rhs)
            total = piece if total is None else total + piece
        for g in range(n.groups):
            piece = total[:, 128 * g : 128 * (g + 1)].astype(BF16).reshape(per_chunk, 16, 128)
            back[pl.ds(chunk * per_chunk, per_chunk), 16 * g : 16 * (g + 1), :] = piece
        return carry

    lax.fori_loop(0, lanes // chunk_rows, gather_chunk, 0)

    def home_to(peer):
        return remote(back.at[peer], home.at[dp], h_send.at[peer], h_recv.at[dp], peer, z)

    def home_from(peer):
        return remote(back.at[peer], home.at[peer], h_send.at[peer], h_recv.at[peer], peer, z)

    peers(lambda peer: home_to(peer).start())
    home[dp] = back[dp]

    swap_k.wait_recv()
    mate_k[...] += kgrad[core]

    def k_rows(at):
        return pl.ds(pl.multiple_of(at * n.krow, 8), n.krow)

    def k_scatter(at, slot):
        return remote(mate_k.at[k_rows(at)], k_in.at[slot], ka_send.at[at], ka_recv.at[slot], 2 * at + core, z)

    def k_over_z(slot, to):
        return remote(k_z.at[z], k_z.at[slot], kz_send.at[to], kz_recv.at[slot], dp, to)

    def k_gather(slot, to):
        return remote(k_all.at[slot], k_all.at[slot], kc_send.at[to], kc_recv.at[slot], 2 * to + core, z)

    chips(lambda at: k_scatter(at, chip).start())

    for step in range(3, far):
        ring_step(step)

    for way, chunk in ((1, 0), (0, 1), (0, 0), (1, 1)):
        steps = ring_steps(way, chunk)
        if steps > 0:
            into = up_in if way == 0 else down_in
            ring_hop(way, chunk, steps - 1).wait_recv()
            part[z, :, chunk_of[chunk]] += into[chunk, steps - 1].astype(F32)

    def along_x(step):
        there = lax.rem(cx + step, n.nx)
        return there, (there * n.ny + cy) * 2 + core

    def along_y(step):
        there = lax.rem(cy + step, n.ny)
        return there, (cx * n.ny + there) * 2 + core

    def x_scatter(step, arriving):
        there, peer = along_x(step)
        slot = there if arriving else cx
        return remote(x_out.at[there], x_in.at[slot], xr_send.at[there], xr_recv.at[slot], peer, z)

    def y_scatter(step, arriving):
        there, peer = along_y(step)
        slot = there if arriving else cy
        return there, remote(y_out.at[there], y_in.at[slot], yr_send.at[there], yr_recv.at[slot], peer, z)

    def y_gather(step, arriving):
        there, peer = along_y(step)
        slot = there if arriving else cy
        return there, remote(y_all.at[slot], y_all.at[slot], yg_send.at[there], yg_recv.at[slot], peer, z)

    def x_gather(step, arriving):
        there, peer = along_x(step)
        slot = there if arriving else cx
        return remote(x_all.at[slot], x_all.at[slot], xg_send.at[there], xg_recv.at[slot], peer, z)

    for i in range(n.nx):
        x_out[i] = part[z, n.prow * i : n.prow * (i + 1), :].astype(BF16)
    for step in range(1, n.nx):
        x_scatter(step, False).start()

    chips(lambda at: k_scatter(chip, at).wait_recv())
    k_in[chip] = mate_k[k_rows(chip), :]

    def k_sum(step, carry):
        return carry + k_in[lax.rem(chip + step, n.chips)]

    k_z[z] = lax.fori_loop(1, n.chips, k_sum, k_in[chip])
    for hop in range(1, n.nz):
        k_over_z(z, lax.rem(z + hop, n.nz)).start()

    band = part[z, pl.ds(pl.multiple_of(cx * n.prow, 16), n.prow), :]
    for step in range(1, n.nx):
        x_scatter(step, True).wait_recv()
        band = band + x_in[lax.rem(cx + step, n.nx)].astype(F32)
    for l in range(n.ltiles):
        y_own[l] = band[:, 128 * l : 128 * (l + 1)]
        y_out[l] = band[:, 128 * l : 128 * (l + 1)].astype(BF16)
    for step in range(1, n.ny):
        there, copy = y_scatter(step, False)

        @pl.when(there < n.ltiles)
        def _():
            copy.start()

    for hop in range(1, n.nz):
        src = lax.rem(z + hop, n.nz)
        k_over_z(src, src).wait_recv()
    small = k_z[0]
    for i in range(1, n.nz):
        small = small + k_z[i]
    k_all[chip] = small * scale
    chips(lambda at: k_gather(chip, at).start())

    @pl.when(cy < n.ltiles)
    def _():
        total = y_own[cy]
        for step in range(1, n.ny):
            there, copy = y_scatter(step, True)
            copy.wait_recv()
            total = total + y_in[there].astype(F32)
        y_all[cy] = (total * scale).astype(BF16)
        for step in range(1, n.ny):
            y_gather(step, False)[1].start()

    for step in range(1, n.ny):
        there, copy = y_gather(step, True)

        @pl.when(there < n.ltiles)
        def _():
            copy.wait_recv()

    for l in range(n.ltiles):
        x_all[cx, :, 128 * l : 128 * (l + 1)] = y_all[l]
    for step in range(1, n.nx):
        x_gather(step, False).start()

    chips(lambda at: k_gather(at, at).wait_recv())
    swap_all = remote(k_all, k_mate, m_send.at[3], m_recv.at[3], mate, z)
    swap_all.start()

    for step in range(1, n.nx):
        x_gather(step, True).wait_recv()
    swap_weight = remote(x_all, x_mate, m_send.at[4], m_recv.at[4], mate, z)
    swap_weight.start()

    def lay_weight(source, half):
        cols = pl.ds(pl.multiple_of(half * n.half, 128), n.half)
        for i in range(n.nx):
            weight_out[n.prow * i : n.prow * (i + 1), cols] = source[i].astype(F32)

    def lay_small(source, half):
        rows = source[...].reshape(n.kall, 128)
        for l in range(n.ltiles):
            cols = pl.ds(pl.multiple_of(half * n.half + 128 * l, 128), 128)
            taps_out[:, cols] = rows[KROWS * l : KROWS * l + TAPS]
            gain_out[:, cols] = rows[KROWS * l + TAPS : KROWS * l + TAPS + 1]
            shift_out[:, cols] = rows[KROWS * l + TAPS + 1 : KROWS * l + TAPS + 2]

    lay_weight(x_all, core)
    lay_small(k_all, core)

    peers(lambda peer: home_from(peer).wait_recv())
    sub_rows = lax.broadcasted_iota(jnp.int32, (n.rows, 1), 0)

    def read_owner(b, carry):
        return jnp.where(sub_rows // BLOCK == b, (dest_ref[b] // n.nb) * 16, carry)

    code_col = lax.fori_loop(0, n.nb, read_owner, jnp.zeros((n.rows, 1), jnp.int32)) + sub_rows % BLOCK
    place = lax.broadcasted_iota(jnp.int32, (n.rows, lanes), 1)
    blocks = jnp.concatenate(
        [home[:, 16 * g : 16 * (g + 1), :].reshape(lanes, 128) for g in range(n.groups)], axis=1
    )
    for jj in range(4):
        rows = dot(one_hot(place == code_col + 4 * jj), blocks).astype(BF16)
        for g in range(n.groups):
            frames_out[:, 128 * (4 * g + jj) : 128 * (4 * g + jj + 1)] = rows[:, 128 * g : 128 * (g + 1)]

    swap_all.wait_recv()
    lay_small(k_mate, other)
    swap_weight.wait_recv()
    lay_weight(x_mate, other)

    for copy in (swap_cot, swap_act, swap_k, swap_all, swap_weight):
        copy.wait_send()
    for step in range(far):
        gather_up(step, z).wait_send()
        gather_down(step, z).wait_send()
        gather_mate(2 * step, z, core).wait_send()
        if step < far - 1:
            gather_mate(2 * step + 1, z, core).wait_send()
    for way in range(2):
        for chunk in range(2):
            for step in range(ring_steps(way, chunk)):
                ring_hop(way, chunk, step).wait_send()
    for step in range(1, n.nx):
        x_scatter(step, False).wait_send()
        x_gather(step, False).wait_send()
    for step in range(1, n.ny):
        there, copy = y_scatter(step, False)

        @pl.when(there < n.ltiles)
        def _():
            copy.wait_send()

    @pl.when(cy < n.ltiles)
    def _():
        for step in range(1, n.ny):
            y_gather(step, False)[1].wait_send()

    for hop in range(1, n.nz):
        k_over_z(z, lax.rem(z + hop, n.nz)).wait_send()

    def small_sent(at):
        k_scatter(at, chip).wait_send()
        k_gather(chip, at).wait_send()

    chips(small_sent)

    def blocks_sent(peer):
        label_to(peer).wait_send()
        block_to(peer).wait_send()
        home_to(peer).wait_send()

    peers(blocks_sent)


def on_device(frames, destination, utt_lengths, cotangent, weight, kernel, norm_gain, norm_shift):
    n = Sizes(lax.axis_size("dp"), lax.axis_size("fsdp"), frames.shape[0], frames.shape[1], weight.shape[0])
    scale = 1.0 / math.sqrt(n.rows * n.nd * n.nz)
    far = n.nz // 2
    vmem = pl.BlockSpec(memory_space=pltpu.VMEM)
    smem = pl.BlockSpec(memory_space=pltpu.SMEM)

    def dma(count):
        return [pltpu.SemaphoreType.DMA((count,))] * 2

    def buf(*shape, dtype=F32):
        return pltpu.VMEM(shape, dtype)

    blocks = buf(n.nb, n.slab, 128, dtype=BF16)
    label = buf(n.nd, 1, 128)
    plane = buf(n.tiles, n.padded, 128)
    ring = buf(2, far, n.shard, n.quarter, dtype=BF16)
    band = buf(n.nx, n.prow, n.half, dtype=BF16)
    tile = buf(n.ny, n.prow, 128, dtype=BF16)
    small = buf(n.chips, n.krow, 128)
    grads = pl.pallas_call(
        functools.partial(module_kernel, n, scale),
        out_shape=(
            jax.ShapeDtypeStruct((n.rows, n.ch), BF16),
            jax.ShapeDtypeStruct((n.shard, n.ch), F32),
            jax.ShapeDtypeStruct((TAPS, n.ch), F32),
            jax.ShapeDtypeStruct((1, n.ch), F32),
            jax.ShapeDtypeStruct((1, n.ch), F32),
        ),
        in_specs=[smem, smem] + [vmem] * 6,
        out_specs=(vmem,) * 5,
        scratch_shapes=[
            blocks, blocks, label, label, buf(16 * n.nb, 128), buf(n.nz, n.shard, n.ch, dtype=BF16),
            plane, plane, plane, plane, plane, buf(n.padded, 128), buf(n.padded, n.ch, dtype=BF16),
            buf(n.tiles, n.padded, 128, dtype=BF16), buf(TAPS, 8, 128), buf(2, n.kall, 128),
            buf(n.padded, n.ch, dtype=BF16), buf(n.ch, 2 * n.rows, dtype=BF16), buf(n.rows, n.ch, dtype=BF16),
            buf(2 * n.rows, n.half, dtype=BF16), buf(n.rows, n.half, dtype=BF16),
            buf(n.nz, n.shard, n.half), ring, ring, ring, ring, blocks, blocks,
            band, band, buf(n.ltiles, n.prow, 128), tile, tile, tile, band, band,
            buf(n.kall, 128), small, buf(n.nz, n.krow, 128), small, small,
            *dma(n.nd), *dma(n.nd), *dma(n.nd),
            *dma(far), *dma(far), *dma(2 * far), *dma(5),
            *dma(2 * far), *dma(2 * far),
            *dma(n.nx), *dma(n.ny), *dma(n.ny), *dma(n.nx),
            *dma(n.chips), *dma(n.nz), *dma(n.chips),
        ],
        compiler_params=pltpu.CompilerParams(
            collective_id=0, has_side_effects=True, vmem_limit_bytes=VMEM_BYTES
        ),
    )(destination, utt_lengths, frames, cotangent, weight, kernel, norm_gain[None, :], norm_shift[None, :])
    return grads[0], grads[1], grads[2], grads[3][0], grads[4][0]


def solution(mesh):
    placed = (
        P(("dp", "fsdp"), None),
        P(("dp", "fsdp")),
        P(("dp", "fsdp"), None),
        P(("dp", "fsdp"), None),
        P("fsdp", None),
        P(),
        P(),
        P(),
    )
    return jax.shard_map(
        on_device,
        mesh=mesh,
        in_specs=placed,
        out_specs=(P(("dp", "fsdp"), None), P("fsdp", None), P(), P(), P()),
        check_vma=False,
    )
```

time: 655 us -> 138 us (0.21)
  waiting for transfers between devices: 404 us -> 0 us
  Pallas kernels: 0 us -> 128 us
  blocking collectives: 100 us -> 0 us
  other arithmetic: 49.2 us -> 2.71 us
  starting transfers between devices: 39.8 us -> 0 us
  local copies, waits for them, and re-layouts: 25.8 us -> 6.45 us
  matrix products: 18.7 us -> 0 us
  between operations: 14.3 us -> 0.65 us
    psum x2 -> x0, waiting for transfers between devices: 383 us -> none  [the longest x1 193 us: on_device(): lax.psum((kernel_part, gain_part, shift_part), ('dp', 'fsdp'))]
    pallas_call x0 -> x1, Pallas kernels: none -> 128 us  [on_device(): pl.pallas_call(functools.partial(module_kernel, n, scale), out_shape=(jax...]
    psum x1 -> x0, blocking collectives: 100 us -> none  [on_device(): lax.psum((kernel_part, gain_part, shift_part), ('dp', 'fsdp'))]
    all_to_all x4 -> x0, starting transfers between devices: 39 us -> none  [the longest x1 11.6 us: on_device(): lax.all_to_all(labels, 'dp', split_axis=0, concat_axis=0, tiled=True)]
    reduce_sum x8 -> x0, other arithmetic: 25.8 us -> none  [the longest x4 12.7 us: on_device(): jnp.sum(grad_filtered * signal_pad[offset:offset + row_count] * inside, a...]
    all_to_all x4 -> x0, waiting for transfers between devices: 20 us -> none  [the longest x1 19.9 us: on_device(): lax.all_to_all(outgoing, 'dp', split_axis=0, concat_axis=0, tiled=True)]
    dot_general x9 -> x0, matrix products: 18.7 us -> none  [the longest x8 12.2 us: on_device(): lax.dot_general(source_cot, source_act, (((0,), (0,)), ((), ())), preferr...]
    scatter x3 -> x0, local copies, waits for them, and re-layouts: 11.4 us -> none  [the longest x1 8.1 us: on_device(): outgoing = jnp.zeros((dp_size * capacity, block_rows, channels), jnp.bflo...]
  transfers between devices with their start and end apart: 8 -> 0, of which waited for: 3 -> 0; matrix products, arithmetic and copies ran while one was open for 13% -> 0% of each run, Pallas kernels for 0% -> 0%
where the time goes in v2:
time: 138 us
  Pallas kernels  128 us (93%)
  local copies, waits for them, and re-layouts  6.45 us (5%)
  other arithmetic  2.71 us (2%)
    pallas_call x1, Pallas kernels, on_device(): pl.pallas_call(functools.partial(module_kernel, n, scale), out_shape=(jax...  128 us
    unnamed x7, local copies, waits for them, and re-layouts  3.86 us

profile of v2, /device:TPU:1, one launch (start us, length us, event | category | flops | bytes accessed | tf_op | source)
XLA Modules:
  0.0 137.5 jit_solution(11550232345575933158)
XLA Ops:
  0.6 1.3 broadcast_in_dim.6.gain_ref
  1.9 1.3 broadcast_in_dim.7.shift_ref
  3.2 127.7 %shard_map.119 = (bf16[256,1536]{1,0:T(8,128)(2,1)}, f32[192,1536]{1,0:T(8,128)}, f32[31,1536]{1,0:T(8,128)}, f32[1,1536]{1,0:T(1,128)}, f32[1,1536]{1,0:T(1,128)}) custom-call(s32[64]{0:T(128)} %dest_ref.1, s32[1,4]{1,0:T(1,128)} %utt_ref.1, bf16[256,1536]{1,0:T(8,128)(2,1)} %frames_ref.1, bf16[256,1536]{1,0:T(8,128)(2,1)} %cot_ref.1, ...), custom_call_target="tpu_custom_call" | custom-call | tf_op jit(solution)/shard_map/pallas_call | solution.py:704
  130.9 0.0 copy-start
  130.9 1.4 %reduce = f32[1536]{0:T(1024)} reduce(f32[1,1536]{1,0:T(1,128)} %get-tuple-element.13, f32[]{:T(128)} %constant.4), dimensions={0}, to_apply=%get-tuple-element.13.reduce_sub_computation | reduce | bytes 12292 | tf_op jit(solution)/shard_map/pallas_call | solution.py:704
  132.4 1.3 reduce.1
  133.7 2.1 %copy.16 = bf16[256,1536]{1,0:T(8,128)(2,1)} copy(bf16[256,1536]{1,0:T(8,128)(2,1)} %get-tuple-element.20) | data formatting | bytes 1572864
  135.7 0.0 copy-done
  135.7 0.0 copy-start.1
  135.7 1.0 copy.17
  136.7 0.1 copy-done.1
  136.8 0.7 copy.18
Async XLA Ops:
  130.9 4.8 %copy-start = (f32[192,1536]{1,0:T(8,128)S(1)}, f32[192,1536]{1,0:T(8,128)}, u32[]{:S(2)}) copy-start(f32[192,1536]{1,0:T(8,128)} %get-tuple-element.21) | copy-start | bytes 3538948
  135.7 1.1 copy-start.1

commit v3 on v2

--- a/solution.py
+++ b/solution.py
@@ -69,7 +69,7 @@
     n, scale,
     dest_ref, utt_ref, frames_ref, cot_ref, weight_ref, taps_ref, gain_ref, shift_ref,
     frames_out, weight_out, taps_out, gain_out, shift_out,
-    outgoing, arrived, label_out, label_in, labels, whole,
+    outgoing, arrived, label_out, label_in, labels, whole, unsort, setting, taking,
     xs, filt, hidden, gf, slope, spread, actp, go, k8, kgrad, cot_pad, cot_turned, mate_cot, act_both, act_send,
     part, up_out, up_in, down_out, down_in, back, home,
     x_out, x_in, y_own, y_out, y_in, y_all, x_all, x_mate, mate_k, k_in, k_z, k_all, k_mate,
@@ -112,27 +112,21 @@
 
     whole[z] = weight_ref[...]
 
-    lane128 = lax.broadcasted_iota(jnp.int32, (1, 128), 1)
     lane_rows = lax.broadcasted_iota(jnp.int32, (1, n.rows), 1)
-
-    def read_block(b, carry):
-        code, owners, slots = carry
-        dest = dest_ref[b]
-        owner = dest // n.nb
-        slot = dest - owner * n.nb
-        code = jnp.where(lane_rows // BLOCK == b, owner * 16, code)
-        owners = jnp.where(lane128 == b, owner, owners)
-        slots = jnp.where(lane128 == b, slot, slots)
-        return code, owners, slots
-
-    start = (jnp.zeros((1, n.rows), jnp.int32), jnp.full((1, 128), -1, jnp.int32), jnp.zeros((1, 128), jnp.int32))
-    code, owners, slots = lax.fori_loop(0, n.nb, read_block, start)
-    code = code + lane_rows % BLOCK
-    owner_iota = lax.broadcasted_iota(jnp.int32, (n.nd, 128), 0)
+    dest = dest_ref[...].reshape(1, n.nb)
+    owners = dest // n.nb
+    slots = dest - owners * n.nb
+    owner_iota = lax.broadcasted_iota(jnp.int32, (n.nd, n.nb), 0)
     slot_of = jnp.sum(jnp.where(owner_iota == owners, slots, 0).astype(F32), axis=1, keepdims=True)
     slot_of = jnp.broadcast_to(slot_of, (n.nd, 128))
     for i in range(n.nd):
         label_out[i] = slot_of[i : i + 1]
+    four = one_hot(
+        lax.broadcasted_iota(jnp.int32, (n.nb, n.rows), 0)
+        == lax.broadcasted_iota(jnp.int32, (n.nb, n.rows), 1) // BLOCK
+    )
+    wide = dot(jnp.broadcast_to(owners.astype(F32), (16, n.nb)).astype(BF16), four)[:1]
+    code = wide.astype(jnp.int32) * 16 + lane_rows % BLOCK
 
     mats = [
         jnp.concatenate(
@@ -242,13 +236,21 @@
     go[...] = jnp.zeros_like(go)
     gf[:, :HALO, :] = jnp.zeros((n.tiles, HALO, 128), F32)
     gf[:, n.padded - HALO :, :] = jnp.zeros((n.tiles, HALO, 128), F32)
+    sub_rows = lax.broadcasted_iota(jnp.int32, (n.rows, 1), 0)
+    near = lax.broadcasted_iota(jnp.int32, (n.rows, n.nb), 1) == sub_rows // BLOCK
+    code_col = jnp.sum(jnp.where(near, owners, 0).astype(F32), axis=1, keepdims=True)
+    code_col = code_col.astype(jnp.int32) * 16 + sub_rows % BLOCK
+    order = lax.broadcasted_iota(jnp.int32, (n.rows, lanes), 1)
+    for jj in range(4):
+        unsort[n.rows * jj : n.rows * (jj + 1)] = one_hot(order == code_col + 4 * jj)
     swap_cot.wait_recv()
     cot_turned[:, n.rows :] = mate_cot[...].T
 
-    for step in range(far - 1):
-        gather_pass(step)
+    if far > 1:
+        gather_pass(0)
 
     peers(lambda peer: label_from(peer).wait_recv())
+    lane128 = lax.broadcasted_iota(jnp.int32, (1, 128), 1)
     chunks = []
     for q in range(n.nb // 8):
         row = jnp.zeros((1, 128), F32)
@@ -265,19 +267,45 @@
 
     lax.fori_loop(0, n.nb, lay_label, 0)
 
+    row_iota = lax.broadcasted_iota(jnp.int32, (n.padded, lanes), 0)
+
+    def setter(jj, carry):
+        mask = row_iota == jnp.where((lane_all // 4) % 4 == jj, place_row, -1)
+        setting[pl.ds(pl.multiple_of(jj * n.padded, 16), n.padded), :] = one_hot(mask)
+        return carry
+
+    lax.fori_loop(0, 4, setter, 0)
+
+    def taker(chunk, carry):
+        at = pl.ds(pl.multiple_of(chunk * chunk_rows, chunk_rows), chunk_rows)
+        slot = labels[at, :][:, :1].astype(jnp.int32)
+        sub = lax.broadcasted_iota(jnp.int32, (chunk_rows, 1), 0)
+        place = padded_place(slot * BLOCK + sub % 4, ends)
+        cols = lax.broadcasted_iota(jnp.int32, (chunk_rows, n.padded), 1)
+        for jj in range(4):
+            taking[jj, at, :] = one_hot(cols == jnp.where((sub // 4) % 4 == jj, place, -1))
+        return carry
+
+    lax.fori_loop(0, lanes // chunk_rows, taker, 0)
+
+    if far > 2:
+        gather_pass(1)
+
     peers(lambda peer: block_from(peer).wait_recv())
     blocks = jnp.concatenate(
         [arrived[:, 16 * g : 16 * (g + 1), :].reshape(lanes, 128) for g in range(n.groups)], axis=1
     )
-    row_iota = lax.broadcasted_iota(jnp.int32, (n.padded, lanes), 0)
 
     def put(jj, carry):
-        owned = dot(one_hot(row_iota == jnp.where((lane_all // 4) % 4 == jj, place_row, -1)), blocks)
+        owned = dot(setting[pl.ds(pl.multiple_of(jj * n.padded, 16), n.padded), :], blocks)
         for g in range(n.groups):
             xs[4 * g + jj] = owned[:, 128 * g : 128 * (g + 1)]
         return carry
 
     lax.fori_loop(0, 4, put, 0)
+
+    for step in range(2, far - 1):
+        gather_pass(step)
 
     def filter_tile(j, carry):
         taps = taps_ref[:, pl.ds(pl.multiple_of(j * 128, 128), 128)]
@@ -294,6 +322,7 @@
         return carry
 
     lax.fori_loop(0, n.tiles, filter_tile, 0)
+    gather_pass(far - 1)
 
     def norm_span(b, carry):
         rows = pl.ds(pl.multiple_of(HALO + n.span * b, 16), n.span)
@@ -310,7 +339,7 @@
         spread[rows, :] = jnp.broadcast_to(inverse, (n.span, 128))
         for j in range(n.tiles):
             whitened = (filt[j, rows, :] - mean) * inverse
-            normed = whitened * gain_ref[:, 128 * j : 128 * (j + 1)] + shift_ref[:, 128 * j : 128 * (j + 1)]
+            normed = whitened * gain_ref[128 * j : 128 * (j + 1)].reshape(1, 128) + shift_ref[128 * j : 128 * (j + 1)].reshape(1, 128)
             logistic = 1.0 / (1.0 + jnp.exp(-normed))
             activated = normed * logistic
             actp[rows, 128 * j : 128 * (j + 1)] = activated.astype(BF16)
@@ -327,7 +356,6 @@
     swap_act.start()
     act_both[: n.rows] = dot(take, actp[:, mine]).astype(BF16)
 
-    gather_pass(far - 1)
     for step in range(far):
         gather_mate(2 * step, below(step) if step < far - 1 else above(step), other).wait_recv()
         if step < far - 1:
@@ -382,15 +410,6 @@
         product(lax.rem(z + n.nz - far + 1, n.nz))
     ring_step(0)
 
-    def products(i, carry):
-        product(lax.rem(z + n.nz - far + 2 + i, n.nz))
-        return carry
-
-    if far > 1:
-        lax.fori_loop(0, n.nz - 3, products, 0)
-    else:
-        product(z)
-
     def norm_back(b, carry):
         rows = pl.ds(pl.multiple_of(HALO + n.span * b, 16), n.span)
         first = jnp.zeros((n.span, 128), F32)
@@ -398,7 +417,7 @@
         for j in range(n.tiles):
             whitened = filt[j, rows, :]
             grad_normed = hidden[j, rows, :] * slope[j, rows, :]
-            scaled = grad_normed * gain_ref[:, 128 * j : 128 * (j + 1)]
+            scaled = grad_normed * gain_ref[128 * j : 128 * (j + 1)].reshape(1, 128)
             hidden[j, rows, :] = scaled
             first = first + scaled
             second = second + scaled * whitened
@@ -413,6 +432,15 @@
         return carry
 
     lax.fori_loop(0, n.used // n.span, norm_back, 0)
+
+    def products(i, carry):
+        product(lax.rem(z + n.nz - far + 2 + i, n.nz))
+        return carry
+
+    if far > 1:
+        lax.fori_loop(0, n.nz - 3, products, 0)
+    else:
+        product(z)
 
     def back_tile(j, carry):
         taps = taps_ref[:, pl.ds(pl.multiple_of(j * 128, 128), 128)]
@@ -450,14 +478,10 @@
 
     def gather_chunk(chunk, carry):
         at = pl.ds(pl.multiple_of(chunk * chunk_rows, chunk_rows), chunk_rows)
-        slot = labels[at, :][:, :1].astype(jnp.int32)
-        sub = lax.broadcasted_iota(jnp.int32, (chunk_rows, 1), 0)
-        place = padded_place(slot * BLOCK + sub % 4, ends)
-        cols = lax.broadcasted_iota(jnp.int32, (chunk_rows, n.padded), 1)
         total = None
         for jj in range(4):
             rhs = jnp.concatenate([go[4 * g + jj] for g in range(n.groups)], axis=1)
-            piece = dot(one_hot(cols == jnp.where((sub // 4) % 4 == jj, place, -1)), rhs)
+            piece = dot(taking[jj, at, :], rhs)
             total = piece if total is None else total + piece
         for g in range(n.groups):
             piece = total[:, 128 * g : 128 * (g + 1)].astype(BF16).reshape(per_chunk, 16, 128)
@@ -494,6 +518,16 @@
 
     for step in range(3, far):
         ring_step(step)
+
+    chips(lambda at: k_scatter(chip, at).wait_recv())
+    k_in[chip] = mate_k[k_rows(chip), :]
+
+    def k_sum(step, carry):
+        return carry + k_in[lax.rem(chip + step, n.chips)]
+
+    k_z[z] = lax.fori_loop(1, n.chips, k_sum, k_in[chip])
+    for hop in range(1, n.nz):
+        k_over_z(z, lax.rem(z + hop, n.nz)).start()
 
     for way, chunk in ((1, 0), (0, 1), (0, 0), (1, 1)):
         steps = ring_steps(way, chunk)
@@ -535,15 +569,14 @@
     for step in range(1, n.nx):
         x_scatter(step, False).start()
 
-    chips(lambda at: k_scatter(chip, at).wait_recv())
-    k_in[chip] = mate_k[k_rows(chip), :]
-
-    def k_sum(step, carry):
-        return carry + k_in[lax.rem(chip + step, n.chips)]
-
-    k_z[z] = lax.fori_loop(1, n.chips, k_sum, k_in[chip])
     for hop in range(1, n.nz):
-        k_over_z(z, lax.rem(z + hop, n.nz)).start()
+        src = lax.rem(z + hop, n.nz)
+        k_over_z(src, src).wait_recv()
+    small = k_z[0]
+    for i in range(1, n.nz):
+        small = small + k_z[i]
+    k_all[chip] = small * scale
+    chips(lambda at: k_gather(chip, at).start())
 
     band = part[z, pl.ds(pl.multiple_of(cx * n.prow, 16), n.prow), :]
     for step in range(1, n.nx):
@@ -558,15 +591,6 @@
         @pl.when(there < n.ltiles)
         def _():
             copy.start()
-
-    for hop in range(1, n.nz):
-        src = lax.rem(z + hop, n.nz)
-        k_over_z(src, src).wait_recv()
-    small = k_z[0]
-    for i in range(1, n.nz):
-        small = small + k_z[i]
-    k_all[chip] = small * scale
-    chips(lambda at: k_gather(chip, at).start())
 
     @pl.when(cy < n.ltiles)
     def _():
@@ -595,6 +619,15 @@
     swap_all = remote(k_all, k_mate, m_send.at[3], m_recv.at[3], mate, z)
     swap_all.start()
 
+    peers(lambda peer: home_from(peer).wait_recv())
+    blocks = jnp.concatenate(
+        [home[:, 16 * g : 16 * (g + 1), :].reshape(lanes, 128) for g in range(n.groups)], axis=1
+    )
+    for jj in range(4):
+        rows = dot(unsort[n.rows * jj : n.rows * (jj + 1)], blocks).astype(BF16)
+        for g in range(n.groups):
+            frames_out[:, 128 * (4 * g + jj) : 128 * (4 * g + jj + 1)] = rows[:, 128 * g : 128 * (g + 1)]
+
     for step in range(1, n.nx):
         x_gather(step, True).wait_recv()
     swap_weight = remote(x_all, x_mate, m_send.at[4], m_recv.at[4], mate, z)
@@ -603,34 +636,18 @@
     def lay_weight(source, half):
         cols = pl.ds(pl.multiple_of(half * n.half, 128), n.half)
         for i in range(n.nx):
-            weight_out[n.prow * i : n.prow * (i + 1), cols] = source[i].astype(F32)
+            weight_out[n.prow * i : n.prow * (i + 1), cols] = source[i]
 
     def lay_small(source, half):
         rows = source[...].reshape(n.kall, 128)
         for l in range(n.ltiles):
             cols = pl.ds(pl.multiple_of(half * n.half + 128 * l, 128), 128)
             taps_out[:, cols] = rows[KROWS * l : KROWS * l + TAPS]
-            gain_out[:, cols] = rows[KROWS * l + TAPS : KROWS * l + TAPS + 1]
-            shift_out[:, cols] = rows[KROWS * l + TAPS + 1 : KROWS * l + TAPS + 2]
+            gain_out[cols] = rows[KROWS * l + TAPS : KROWS * l + TAPS + 1].reshape(128)
+            shift_out[cols] = rows[KROWS * l + TAPS + 1 : KROWS * l + TAPS + 2].reshape(128)
 
     lay_weight(x_all, core)
     lay_small(k_all, core)
-
-    peers(lambda peer: home_from(peer).wait_recv())
-    sub_rows = lax.broadcasted_iota(jnp.int32, (n.rows, 1), 0)
-
-    def read_owner(b, carry):
-        return jnp.where(sub_rows // BLOCK == b, (dest_ref[b] // n.nb) * 16, carry)
-
-    code_col = lax.fori_loop(0, n.nb, read_owner, jnp.zeros((n.rows, 1), jnp.int32)) + sub_rows % BLOCK
-    place = lax.broadcasted_iota(jnp.int32, (n.rows, lanes), 1)
-    blocks = jnp.concatenate(
-        [home[:, 16 * g : 16 * (g + 1), :].reshape(lanes, 128) for g in range(n.groups)], axis=1
-    )
-    for jj in range(4):
-        rows = dot(one_hot(place == code_col + 4 * jj), blocks).astype(BF16)
-        for g in range(n.groups):
-            frames_out[:, 128 * (4 * g + jj) : 128 * (4 * g + jj + 1)] = rows[:, 128 * g : 128 * (g + 1)]
 
     swap_all.wait_recv()
     lay_small(k_mate, other)
@@ -685,6 +702,7 @@
     n = Sizes(lax.axis_size("dp"), lax.axis_size("fsdp"), frames.shape[0], frames.shape[1], weight.shape[0])
     scale = 1.0 / math.sqrt(n.rows * n.nd * n.nz)
     far = n.nz // 2
+    lanes = 16 * n.nb
     vmem = pl.BlockSpec(memory_space=pltpu.VMEM)
     smem = pl.BlockSpec(memory_space=pltpu.SMEM)
 
@@ -705,15 +723,16 @@
         functools.partial(module_kernel, n, scale),
         out_shape=(
             jax.ShapeDtypeStruct((n.rows, n.ch), BF16),
-            jax.ShapeDtypeStruct((n.shard, n.ch), F32),
+            jax.ShapeDtypeStruct((n.shard, n.ch), BF16),
             jax.ShapeDtypeStruct((TAPS, n.ch), F32),
-            jax.ShapeDtypeStruct((1, n.ch), F32),
-            jax.ShapeDtypeStruct((1, n.ch), F32),
+            jax.ShapeDtypeStruct((n.ch,), F32),
+            jax.ShapeDtypeStruct((n.ch,), F32),
         ),
-        in_specs=[smem, smem] + [vmem] * 6,
+        in_specs=[vmem, smem] + [vmem] * 6,
         out_specs=(vmem,) * 5,
         scratch_shapes=[
             blocks, blocks, label, label, buf(16 * n.nb, 128), buf(n.nz, n.shard, n.ch, dtype=BF16),
+            buf(4 * n.rows, lanes, dtype=BF16), buf(4 * n.padded, lanes, dtype=BF16), buf(4, lanes, n.padded, dtype=BF16),
             plane, plane, plane, plane, plane, buf(n.padded, 128), buf(n.padded, n.ch, dtype=BF16),
             buf(n.tiles, n.padded, 128, dtype=BF16), buf(TAPS, 8, 128), buf(2, n.kall, 128),
             buf(n.padded, n.ch, dtype=BF16), buf(n.ch, 2 * n.rows, dtype=BF16), buf(n.rows, n.ch, dtype=BF16),
@@ -730,8 +749,8 @@
         compiler_params=pltpu.CompilerParams(
             collective_id=0, has_side_effects=True, vmem_limit_bytes=VMEM_BYTES
         ),
-    )(destination, utt_lengths, frames, cotangent, weight, kernel, norm_gain[None, :], norm_shift[None, :])
-    return grads[0], grads[1], grads[2], grads[3][0], grads[4][0]
+    )(destination, utt_lengths, frames, cotangent, weight, kernel, norm_gain, norm_shift)
+    return grads[0], grads[1].astype(F32), grads[2], grads[3], grads[4]
 
 
 def solution(mesh):

time: 138 us -> 141 us (1.022)
  Pallas kernels: 128 us -> 135 us
  local copies, waits for them, and re-layouts: 6.45 us -> 2.97 us
    pallas_call x1, Pallas kernels: 128 us -> 135 us  [on_device(): pl.pallas_call(functools.partial(module_kernel, n, scale), out_shape=(jax...]
    pallas_call x2 -> x0, other arithmetic: 2.71 us -> none  [on_device(): pl.pallas_call(functools.partial(module_kernel, n, scale), out_shape=(jax...]
    broadcast_in_dim x2 -> x0, local copies, waits for them, and re-layouts: 2.59 us -> none  [the longest x1 1.3 us: on_device(): norm_gain[None, :]]
    convert_element_type x0 -> x1, other arithmetic: none -> 2.28 us  [on_device(): return (grads[0], grads[1].astype(F32), grads[2], grads[3], grads[4])]
    unnamed x7 -> x12, local copies, waits for them, and re-layouts: 3.86 us -> 2.97 us
where the time goes in v3:
time: 141 us
  Pallas kernels  135 us (96%)
  local copies, waits for them, and re-layouts  2.97 us (2%)
  other arithmetic  2.28 us (2%)
    pallas_call x1, Pallas kernels, on_device(): pl.pallas_call(functools.partial(module_kernel, n, scale), out_shape=(jax...  135 us
    unnamed x12, local copies, waits for them, and re-layouts  2.97 us

profile of v3, /device:TPU:1, one launch (start us, length us, event | category | flops | bytes accessed | tf_op | source)
XLA Modules:
  0.0 141.2 jit_solution(12865380567330434321)
XLA Ops:
  0.6 135.3 %shard_map.119 = (bf16[256,1536]{1,0:T(8,128)(2,1)}, bf16[192,1536]{1,0:T(8,128)(2,1)}, f32[31,1536]{1,0:T(8,128)}, f32[1536]{0:T(1024)}, f32[1536]{0:T(1024)}) custom-call(s32[64]{0:T(128)} %dest_ref.1, s32[1,4]{1,0:T(1,128)} %utt_ref.1, bf16[256,1536]{1,0:T(8,128)(2,1)} %frames_ref.1, bf16[256,1536]{1,0:T(8,128)(2,1)} %cot_ref.1, ...), custom_call_target="tpu_custom_call" | custom-call | tf_op jit(solution)/shard_map/pallas_call | solution.py:722
  135.9 0.0 copy-start
  135.9 2.3 %convert_element_type.3 = f32[192,1536]{1,0:T(8,128)} convert(bf16[192,1536]{1,0:T(8,128)(2,1)} %get-tuple-element.11) | non-fusion elementwise | flops 294912 | bytes 1769472 | tf_op jit(solution)/shard_map/convert_element_type | solution.py:753
  138.2 0.0 copy-done
  138.2 0.0 copy-start.1
  138.2 0.0 copy-start.3
  138.2 0.0 copy-start.2
  138.2 0.9 copy.17
  139.1 0.2 copy-done.1
  139.3 0.7 copy.18
  140.0 0.0 copy-done.3
  140.0 0.6 copy.19
  140.6 0.0 copy-done.2
  140.6 0.6 copy.20
Async XLA Ops:
  135.9 2.3 %copy-start = (bf16[256,1536]{1,0:T(8,128)(2,1)S(1)}, bf16[256,1536]{1,0:T(8,128)(2,1)}, u32[]{:S(2)}) copy-start(bf16[256,1536]{1,0:T(8,128)(2,1)} %get-tuple-element.20) | copy-start | bytes 2359300
  138.2 1.1 copy-start.1
  138.2 1.8 %copy-start.3 = (f32[1536]{0:T(1024)S(1)}, f32[1536]{0:T(1024)}, u32[]{:S(2)}) copy-start(f32[1536]{0:T(1024)} %get-tuple-element.23) | copy-start | bytes 18436
  138.2 2.4 %copy-start.2 = (f32[1536]{0:T(1024)S(1)}, f32[1536]{0:T(1024)}, u32[]{:S(2)}) copy-start(f32[1536]{0:T(1024)} %get-tuple-element.24) | copy-start | bytes 18436

commit v4 on v3

--- a/solution.py
+++ b/solution.py
@@ -58,6 +58,11 @@
     )
 
 
+def await_bytes(ref, count, sem):
+    part = ref.at[pl.ds(0, count)]
+    pltpu.make_async_copy(part, part, sem).wait()
+
+
 def padded_place(frame, ends):
     place = frame + HALO
     for end in ends:
@@ -67,13 +72,14 @@
 
 def module_kernel(
     n, scale,
-    dest_ref, utt_ref, frames_ref, cot_ref, weight_ref, taps_ref, gain_ref, shift_ref,
+    dest_ref, utt_ref, frames_hbm, cot_hbm, weight_hbm, taps_ref, gain_ref, shift_ref,
     frames_out, weight_out, taps_out, gain_out, shift_out,
+    frames_ref, cot_ref,
     outgoing, arrived, label_out, label_in, labels, whole, unsort, setting, taking,
     xs, filt, hidden, gf, slope, spread, actp, go, k8, kgrad, cot_pad, cot_turned, mate_cot, act_both, act_send,
     part, up_out, up_in, down_out, down_in, back, home,
     x_out, x_in, y_own, y_out, y_in, y_all, x_all, x_mate, mate_k, k_in, k_z, k_all, k_mate,
-    b_send, b_recv, l_send, l_recv, h_send, h_recv,
+    io, b_send, b_recv, l_send, l_recv, h_send, h_recv,
     gu_send, gu_recv, gd_send, gd_recv, gm_send, gm_recv, m_send, m_recv,
     u_send, u_recv, d_send, d_recv,
     xr_send, xr_recv, yr_send, yr_recv, yg_send, yg_recv, xg_send, xg_recv,
@@ -96,6 +102,14 @@
     mine = pl.ds(pl.multiple_of(core * n.half, 128), n.half)
     theirs = pl.ds(pl.multiple_of(other * n.half, 128), n.half)
 
+    loads = [
+        pltpu.make_async_copy(frames_hbm, frames_ref, io.at[0]),
+        pltpu.make_async_copy(weight_hbm, whole.at[z], io.at[1]),
+        pltpu.make_async_copy(cot_hbm, cot_ref, io.at[2]),
+    ]
+    for load in loads:
+        load.start()
+
     barrier = pltpu.get_barrier_semaphore()
 
     def along_dp(step, carry):
@@ -109,8 +123,6 @@
         pl.semaphore_signal(
             barrier, inc=1, device_id=(dp, lax.rem(z + step, n.nz)), device_id_type=MESH
         )
-
-    whole[z] = weight_ref[...]
 
     lane_rows = lax.broadcasted_iota(jnp.int32, (1, n.rows), 1)
     dest = dest_ref[...].reshape(1, n.nb)
@@ -128,6 +140,7 @@
     wide = dot(jnp.broadcast_to(owners.astype(F32), (16, n.nb)).astype(BF16), four)[:1]
     code = wide.astype(jnp.int32) * 16 + lane_rows % BLOCK
 
+    loads[0].wait()
     mats = [
         jnp.concatenate(
             [frames_ref[:, 128 * (4 * g + jj) : 128 * (4 * g + jj + 1)] for g in range(n.groups)], axis=1
@@ -149,6 +162,7 @@
 
     lax.fori_loop(0, lanes // chunk_rows, sort_chunk, 0)
 
+    loads[1].wait()
     pl.semaphore_wait(barrier, n.nd - 1 + n.nz - 1)
 
     def gather_hop(step, block, first, count, to, send, recv):
@@ -163,9 +177,9 @@
         last = step == far - 1
         return gather_hop(step, block, hrow // 2 if last else 0, hrow // 2 if last else hrow, down, gd_send, gd_recv)
 
-    def gather_mate(slot, block, half):
+    def gather_mate(block, half):
         rows = pl.ds(pl.multiple_of(half * hrow, 16), hrow)
-        return remote(whole.at[block, rows], whole.at[block, rows], gm_send.at[slot], gm_recv.at[slot], mate, z)
+        return remote(whole.at[block, rows], whole.at[block, rows], gm_send.at[0], gm_recv.at[0], mate, z)
 
     def below(step):
         return lax.rem(z + n.nz - step - 1, n.nz)
@@ -177,28 +191,22 @@
         gather_up(step, below(step)).wait_recv()
         if step < far - 1:
             gather_up(step + 1, below(step)).start()
-            gather_mate(2 * step, below(step), core).start()
+            gather_mate(below(step), core).start()
         gather_down(step, above(step)).wait_recv()
         if step < far - 1:
             gather_down(step + 1, above(step)).start()
-            gather_mate(2 * step + 1, above(step), core).start()
+            gather_mate(above(step), core).start()
         else:
-            gather_mate(2 * step, above(step), core).start()
+            gather_mate(above(step), core).start()
 
     gather_up(0, z).start()
     gather_down(0, z).start()
 
     def block_to(peer):
-        return remote(outgoing.at[peer], arrived.at[dp], b_send.at[peer], b_recv.at[dp], peer, z)
-
-    def block_from(peer):
-        return remote(outgoing.at[peer], arrived.at[peer], b_send.at[peer], b_recv.at[peer], peer, z)
+        return remote(outgoing.at[peer], arrived.at[dp], b_send.at[0], b_recv.at[0], peer, z)
 
     def label_to(peer):
-        return remote(label_out.at[peer], label_in.at[dp], l_send.at[peer], l_recv.at[dp], peer, z)
-
-    def label_from(peer):
-        return remote(label_out.at[peer], label_in.at[peer], l_send.at[peer], l_recv.at[peer], peer, z)
+        return remote(label_out.at[peer], label_in.at[dp], l_send.at[0], l_recv.at[0], peer, z)
 
     def peers(body):
         def step_to(step, carry):
@@ -219,6 +227,7 @@
         block_to(peer).start()
 
     peers(send_block)
+    loads[2].wait()
     swap_cot = remote(cot_ref, mate_cot, m_send.at[0], m_recv.at[0], mate, z)
     swap_cot.start()
     arrived[dp] = outgoing[dp]
@@ -249,7 +258,7 @@
     if far > 1:
         gather_pass(0)
 
-    peers(lambda peer: label_from(peer).wait_recv())
+    await_bytes(label_in, n.nd - 1, l_recv.at[0])
     lane128 = lax.broadcasted_iota(jnp.int32, (1, 128), 1)
     chunks = []
     for q in range(n.nb // 8):
@@ -291,7 +300,7 @@
     if far > 2:
         gather_pass(1)
 
-    peers(lambda peer: block_from(peer).wait_recv())
+    await_bytes(arrived, n.nd - 1, b_recv.at[0])
     blocks = jnp.concatenate(
         [arrived[:, 16 * g : 16 * (g + 1), :].reshape(lanes, 128) for g in range(n.groups)], axis=1
     )
@@ -356,10 +365,7 @@
     swap_act.start()
     act_both[: n.rows] = dot(take, actp[:, mine]).astype(BF16)
 
-    for step in range(far):
-        gather_mate(2 * step, below(step) if step < far - 1 else above(step), other).wait_recv()
-        if step < far - 1:
-            gather_mate(2 * step + 1, above(step), other).wait_recv()
+    await_bytes(whole.at[:, pl.ds(0, hrow)], n.nz - 1, gm_recv.at[0])
     width = 512
     per = width // 128
 
@@ -491,35 +497,33 @@
     lax.fori_loop(0, lanes // chunk_rows, gather_chunk, 0)
 
     def home_to(peer):
-        return remote(back.at[peer], home.at[dp], h_send.at[peer], h_recv.at[dp], peer, z)
-
-    def home_from(peer):
-        return remote(back.at[peer], home.at[peer], h_send.at[peer], h_recv.at[peer], peer, z)
+        return remote(back.at[peer], home.at[dp], h_send.at[0], h_recv.at[0], peer, z)
+
+    swap_k.wait_recv()
+    mate_k[...] += kgrad[core]
+
+    def k_rows(at):
+        return pl.ds(pl.multiple_of(at * n.krow, 8), n.krow)
+
+    def k_scatter(at, slot):
+        return remote(mate_k.at[k_rows(at)], k_in.at[slot], ka_send.at[0], ka_recv.at[0], 2 * at + core, z)
+
+    def k_over_z(slot, to):
+        return remote(k_z.at[z], k_z.at[slot], kz_send.at[0], kz_recv.at[0], dp, to)
+
+    def k_gather(slot, to):
+        return remote(k_all.at[slot], k_all.at[slot], kc_send.at[0], kc_recv.at[0], 2 * to + core, z)
+
+    chips(lambda at: k_scatter(at, chip).start())
 
     peers(lambda peer: home_to(peer).start())
     home[dp] = back[dp]
 
-    swap_k.wait_recv()
-    mate_k[...] += kgrad[core]
-
-    def k_rows(at):
-        return pl.ds(pl.multiple_of(at * n.krow, 8), n.krow)
-
-    def k_scatter(at, slot):
-        return remote(mate_k.at[k_rows(at)], k_in.at[slot], ka_send.at[at], ka_recv.at[slot], 2 * at + core, z)
-
-    def k_over_z(slot, to):
-        return remote(k_z.at[z], k_z.at[slot], kz_send.at[to], kz_recv.at[slot], dp, to)
-
-    def k_gather(slot, to):
-        return remote(k_all.at[slot], k_all.at[slot], kc_send.at[to], kc_recv.at[slot], 2 * to + core, z)
-
-    chips(lambda at: k_scatter(at, chip).start())
 
     for step in range(3, far):
         ring_step(step)
 
-    chips(lambda at: k_scatter(chip, at).wait_recv())
+    await_bytes(k_in, n.chips - 1, ka_recv.at[0])
     k_in[chip] = mate_k[k_rows(chip), :]
 
     def k_sum(step, carry):
@@ -544,34 +548,28 @@
         there = lax.rem(cy + step, n.ny)
         return there, (cx * n.ny + there) * 2 + core
 
-    def x_scatter(step, arriving):
+    def x_scatter(step):
         there, peer = along_x(step)
-        slot = there if arriving else cx
-        return remote(x_out.at[there], x_in.at[slot], xr_send.at[there], xr_recv.at[slot], peer, z)
-
-    def y_scatter(step, arriving):
+        return remote(x_out.at[there], x_in.at[cx], xr_send.at[0], xr_recv.at[0], peer, z)
+
+    def y_scatter(step):
         there, peer = along_y(step)
-        slot = there if arriving else cy
-        return there, remote(y_out.at[there], y_in.at[slot], yr_send.at[there], yr_recv.at[slot], peer, z)
-
-    def y_gather(step, arriving):
+        return there, remote(y_out.at[there], y_in.at[cy], yr_send.at[0], yr_recv.at[0], peer, z)
+
+    def y_gather(step):
         there, peer = along_y(step)
-        slot = there if arriving else cy
-        return there, remote(y_all.at[slot], y_all.at[slot], yg_send.at[there], yg_recv.at[slot], peer, z)
-
-    def x_gather(step, arriving):
+        return remote(y_all.at[cy], y_all.at[cy], yg_send.at[0], yg_recv.at[0], peer, z)
+
+    def x_gather(step):
         there, peer = along_x(step)
-        slot = there if arriving else cx
-        return remote(x_all.at[slot], x_all.at[slot], xg_send.at[there], xg_recv.at[slot], peer, z)
+        return remote(x_all.at[cx], x_all.at[cx], xg_send.at[0], xg_recv.at[0], peer, z)
 
     for i in range(n.nx):
         x_out[i] = part[z, n.prow * i : n.prow * (i + 1), :].astype(BF16)
     for step in range(1, n.nx):
-        x_scatter(step, False).start()
-
-    for hop in range(1, n.nz):
-        src = lax.rem(z + hop, n.nz)
-        k_over_z(src, src).wait_recv()
+        x_scatter(step).start()
+
+    await_bytes(k_z, n.nz - 1, kz_recv.at[0])
     small = k_z[0]
     for i in range(1, n.nz):
         small = small + k_z[i]
@@ -579,14 +577,14 @@
     chips(lambda at: k_gather(chip, at).start())
 
     band = part[z, pl.ds(pl.multiple_of(cx * n.prow, 16), n.prow), :]
+    await_bytes(x_in, n.nx - 1, xr_recv.at[0])
     for step in range(1, n.nx):
-        x_scatter(step, True).wait_recv()
         band = band + x_in[lax.rem(cx + step, n.nx)].astype(F32)
     for l in range(n.ltiles):
         y_own[l] = band[:, 128 * l : 128 * (l + 1)]
         y_out[l] = band[:, 128 * l : 128 * (l + 1)].astype(BF16)
     for step in range(1, n.ny):
-        there, copy = y_scatter(step, False)
+        there, copy = y_scatter(step)
 
         @pl.when(there < n.ltiles)
         def _():
@@ -594,42 +592,46 @@
 
     @pl.when(cy < n.ltiles)
     def _():
+        await_bytes(y_in, n.ny - 1, yr_recv.at[0])
         total = y_own[cy]
         for step in range(1, n.ny):
-            there, copy = y_scatter(step, True)
-            copy.wait_recv()
-            total = total + y_in[there].astype(F32)
+            total = total + y_in[lax.rem(cy + step, n.ny)].astype(F32)
         y_all[cy] = (total * scale).astype(BF16)
         for step in range(1, n.ny):
-            y_gather(step, False)[1].start()
-
-    for step in range(1, n.ny):
-        there, copy = y_gather(step, True)
-
-        @pl.when(there < n.ltiles)
+            y_gather(step).start()
+
+    def others_along_y(ref, sem):
+        @pl.when(cy < n.ltiles)
         def _():
-            copy.wait_recv()
+            await_bytes(ref, n.ltiles - 1, sem)
+
+        @pl.when(cy >= n.ltiles)
+        def _():
+            await_bytes(ref, n.ltiles, sem)
+
+    others_along_y(y_all, yg_recv.at[0])
 
     for l in range(n.ltiles):
         x_all[cx, :, 128 * l : 128 * (l + 1)] = y_all[l]
     for step in range(1, n.nx):
-        x_gather(step, False).start()
-
-    chips(lambda at: k_gather(at, at).wait_recv())
+        x_gather(step).start()
+
+    await_bytes(k_all, n.chips - 1, kc_recv.at[0])
     swap_all = remote(k_all, k_mate, m_send.at[3], m_recv.at[3], mate, z)
     swap_all.start()
 
-    peers(lambda peer: home_from(peer).wait_recv())
+    await_bytes(home, n.nd - 1, h_recv.at[0])
     blocks = jnp.concatenate(
         [home[:, 16 * g : 16 * (g + 1), :].reshape(lanes, 128) for g in range(n.groups)], axis=1
     )
     for jj in range(4):
         rows = dot(unsort[n.rows * jj : n.rows * (jj + 1)], blocks).astype(BF16)
         for g in range(n.groups):
-            frames_out[:, 128 * (4 * g + jj) : 128 * (4 * g + jj + 1)] = rows[:, 128 * g : 128 * (g + 1)]
-
-    for step in range(1, n.nx):
-        x_gather(step, True).wait_recv()
+            frames_ref[:, 128 * (4 * g + jj) : 128 * (4 * g + jj + 1)] = rows[:, 128 * g : 128 * (g + 1)]
+    store = pltpu.make_async_copy(frames_ref, frames_out, io.at[3])
+    store.start()
+
+    await_bytes(x_all, n.nx - 1, xg_recv.at[0])
     swap_weight = remote(x_all, x_mate, m_send.at[4], m_recv.at[4], mate, z)
     swap_weight.start()
 
@@ -659,43 +661,26 @@
     for step in range(far):
         gather_up(step, z).wait_send()
         gather_down(step, z).wait_send()
-        gather_mate(2 * step, z, core).wait_send()
-        if step < far - 1:
-            gather_mate(2 * step + 1, z, core).wait_send()
     for way in range(2):
         for chunk in range(2):
             for step in range(ring_steps(way, chunk)):
                 ring_hop(way, chunk, step).wait_send()
-    for step in range(1, n.nx):
-        x_scatter(step, False).wait_send()
-        x_gather(step, False).wait_send()
-    for step in range(1, n.ny):
-        there, copy = y_scatter(step, False)
-
-        @pl.when(there < n.ltiles)
-        def _():
-            copy.wait_send()
+    await_bytes(x_in, n.nx - 1, xr_send.at[0])
+    await_bytes(x_all, n.nx - 1, xg_send.at[0])
+    others_along_y(y_out, yr_send.at[0])
 
     @pl.when(cy < n.ltiles)
     def _():
-        for step in range(1, n.ny):
-            y_gather(step, False)[1].wait_send()
-
-    for hop in range(1, n.nz):
-        k_over_z(z, lax.rem(z + hop, n.nz)).wait_send()
-
-    def small_sent(at):
-        k_scatter(at, chip).wait_send()
-        k_gather(chip, at).wait_send()
-
-    chips(small_sent)
-
-    def blocks_sent(peer):
-        label_to(peer).wait_send()
-        block_to(peer).wait_send()
-        home_to(peer).wait_send()
-
-    peers(blocks_sent)
+        await_bytes(y_all, n.ny - 1, yg_send.at[0])
+
+    await_bytes(whole.at[:, pl.ds(0, hrow)], n.nz - 1, gm_send.at[0])
+    await_bytes(k_z, n.nz - 1, kz_send.at[0])
+    await_bytes(k_in, n.chips - 1, ka_send.at[0])
+    await_bytes(k_all, n.chips - 1, kc_send.at[0])
+    await_bytes(label_out, n.nd - 1, l_send.at[0])
+    await_bytes(outgoing, n.nd - 1, b_send.at[0])
+    await_bytes(back, n.nd - 1, h_send.at[0])
+    store.wait()
 
 
 def on_device(frames, destination, utt_lengths, cotangent, weight, kernel, norm_gain, norm_shift):
@@ -705,6 +690,7 @@
     lanes = 16 * n.nb
     vmem = pl.BlockSpec(memory_space=pltpu.VMEM)
     smem = pl.BlockSpec(memory_space=pltpu.SMEM)
+    hbm = pl.BlockSpec(memory_space=pl.ANY)
 
     def dma(count):
         return [pltpu.SemaphoreType.DMA((count,))] * 2
@@ -728,9 +714,10 @@
             jax.ShapeDtypeStruct((n.ch,), F32),
             jax.ShapeDtypeStruct((n.ch,), F32),
         ),
-        in_specs=[vmem, smem] + [vmem] * 6,
-        out_specs=(vmem,) * 5,
+        in_specs=[vmem, smem, hbm, hbm, hbm, vmem, vmem, vmem],
+        out_specs=(hbm, vmem, vmem, vmem, vmem),
         scratch_shapes=[
+            buf(n.rows, n.ch, dtype=BF16), buf(n.rows, n.ch, dtype=BF16),
             blocks, blocks, label, label, buf(16 * n.nb, 128), buf(n.nz, n.shard, n.ch, dtype=BF16),
             buf(4 * n.rows, lanes, dtype=BF16), buf(4 * n.padded, lanes, dtype=BF16), buf(4, lanes, n.padded, dtype=BF16),
             plane, plane, plane, plane, plane, buf(n.padded, 128), buf(n.padded, n.ch, dtype=BF16),
@@ -740,11 +727,11 @@
             buf(n.nz, n.shard, n.half), ring, ring, ring, ring, blocks, blocks,
             band, band, buf(n.ltiles, n.prow, 128), tile, tile, tile, band, band,
             buf(n.kall, 128), small, buf(n.nz, n.krow, 128), small, small,
-            *dma(n.nd), *dma(n.nd), *dma(n.nd),
-            *dma(far), *dma(far), *dma(2 * far), *dma(5),
+            pltpu.SemaphoreType.DMA((4,)), *dma(1), *dma(1), *dma(1),
+            *dma(far), *dma(far), *dma(1), *dma(5),
             *dma(2 * far), *dma(2 * far),
-            *dma(n.nx), *dma(n.ny), *dma(n.ny), *dma(n.nx),
-            *dma(n.chips), *dma(n.nz), *dma(n.chips),
+            *dma(1), *dma(1), *dma(1), *dma(1),
+            *dma(1), *dma(1), *dma(1),
         ],
         compiler_params=pltpu.CompilerParams(
             collective_id=0, has_side_effects=True, vmem_limit_bytes=VMEM_BYTES

time: 141 us -> 124 us (0.88)
  Pallas kernels: 135 us -> 118 us
    pallas_call x1, Pallas kernels: 135 us -> 118 us  [on_device(): pl.pallas_call(functools.partial(module_kernel, n, scale), out_shape=(jax...]
where the time goes in v4:
time: 124 us
  Pallas kernels  118 us (95%)
  local copies, waits for them, and re-layouts  2.97 us (2%)
  other arithmetic  2.28 us (2%)
    pallas_call x1, Pallas kernels, on_device(): pl.pallas_call(functools.partial(module_kernel, n, scale), out_shape=(jax...  118 us
    unnamed x12, local copies, waits for them, and re-layouts  2.97 us

profile of v4, /device:TPU:1, one launch (start us, length us, event | category | flops | bytes accessed | tf_op | source)
XLA Modules:
  0.0 123.6 jit_solution(12052162954086781012)
XLA Ops:
  0.6 117.7 %shard_map.119 = (bf16[256,1536]{1,0:T(8,128)(2,1)}, bf16[192,1536]{1,0:T(8,128)(2,1)}, f32[31,1536]{1,0:T(8,128)}, f32[1536]{0:T(1024)}, f32[1536]{0:T(1024)}) custom-call(s32[64]{0:T(128)} %dest_ref.1, s32[1,4]{1,0:T(1,128)} %utt_ref.1, bf16[256,1536]{1,0:T(8,128)(2,1)} %frames_hbm.1, bf16[256,1536]{1,0:T(8,128)(2,1)} %cot_hbm.1, ...), custom_call_target="tpu_custom_call" | custom-call | tf_op jit(solution)/shard_map/pallas_call | solution.py:708
  118.4 0.0 copy-start
  118.4 2.3 %convert_element_type.3 = f32[192,1536]{1,0:T(8,128)} convert(bf16[192,1536]{1,0:T(8,128)(2,1)} %get-tuple-element.11) | non-fusion elementwise | flops 294912 | bytes 1769472 | tf_op jit(solution)/shard_map/convert_element_type | solution.py:740
  120.6 0.0 copy-done
  120.7 0.0 copy-start.1
  120.7 0.0 copy-start.3
  120.7 0.0 copy-start.2
  120.7 0.9 copy.17
  121.5 0.2 copy-done.1
  121.7 0.7 copy.18
  122.4 0.0 copy-done.3
  122.4 0.6 copy.19
  123.0 0.0 copy-done.2
  123.0 0.6 copy.20
Async XLA Ops:
  118.4 2.3 %copy-start = (bf16[256,1536]{1,0:T(8,128)(2,1)S(1)}, bf16[256,1536]{1,0:T(8,128)(2,1)}, u32[]{:S(2)}) copy-start(bf16[256,1536]{1,0:T(8,128)(2,1)} %get-tuple-element.20) | copy-start | bytes 2359300
  120.7 1.1 copy-start.1
  120.7 1.8 %copy-start.3 = (f32[1536]{0:T(1024)S(1)}, f32[1536]{0:T(1024)}, u32[]{:S(2)}) copy-start(f32[1536]{0:T(1024)} %get-tuple-element.23) | copy-start | bytes 18436
  120.7 2.4 %copy-start.2 = (f32[1536]{0:T(1024)S(1)}, f32[1536]{0:T(1024)}, u32[]{:S(2)}) copy-start(f32[1536]{0:T(1024)} %get-tuple-element.24) | copy-start | bytes 18436

commit v5 on v4

--- a/solution.py
+++ b/solution.py
@@ -73,7 +73,7 @@
 def module_kernel(
     n, scale,
     dest_ref, utt_ref, frames_hbm, cot_hbm, weight_hbm, taps_ref, gain_ref, shift_ref,
-    frames_out, weight_out, taps_out, gain_out, shift_out,
+    frames_out, weight_out, small_out,
     frames_ref, cot_ref,
     outgoing, arrived, label_out, label_in, labels, whole, unsort, setting, taking,
     xs, filt, hidden, gf, slope, spread, actp, go, k8, kgrad, cot_pad, cot_turned, mate_cot, act_both, act_send,
@@ -165,42 +165,38 @@
     loads[1].wait()
     pl.semaphore_wait(barrier, n.nd - 1 + n.nz - 1)
 
-    def gather_hop(step, block, first, count, to, send, recv):
-        rows = pl.ds(pl.multiple_of(core * hrow + first, 16), count)
-        return remote(whole.at[block, rows], whole.at[block, rows], send.at[step], recv.at[step], dp, to)
-
-    def gather_up(step, block):
-        last = step == far - 1
-        return gather_hop(step, block, 0, hrow // 2 if last else hrow, up, gu_send, gu_recv)
-
-    def gather_down(step, block):
-        last = step == far - 1
-        return gather_hop(step, block, hrow // 2 if last else 0, hrow // 2 if last else hrow, down, gd_send, gd_recv)
-
-    def gather_mate(block, half):
-        rows = pl.ds(pl.multiple_of(half * hrow, 16), hrow)
+    hchunk = hrow // 2
+
+    def gather_hop(way, chunk, step, block):
+        send, recv, to = (gu_send, gu_recv, up) if way == 0 else (gd_send, gd_recv, down)
+        rows = pl.ds(pl.multiple_of(core * hrow + chunk * hchunk, 16), hchunk)
+        at = far * chunk + step
+        return remote(whole.at[block, rows], whole.at[block, rows], send.at[at], recv.at[at], dp, to)
+
+    def gather_mate(chunk, block):
+        rows = pl.ds(pl.multiple_of(core * hrow + chunk * hchunk, 16), hchunk)
         return remote(whole.at[block, rows], whole.at[block, rows], gm_send.at[0], gm_recv.at[0], mate, z)
 
-    def below(step):
-        return lax.rem(z + n.nz - step - 1, n.nz)
-
-    def above(step):
-        return lax.rem(z + step + 1, n.nz)
+    def gather_block(way, step):
+        return lax.rem(z + n.nz - step - 1, n.nz) if way == 0 else lax.rem(z + step + 1, n.nz)
+
+    ways = ((0, 0), (1, 1), (0, 1), (1, 0))
+
+    def ring_steps(way, chunk):
+        return far if way == chunk else far - 1
 
     def gather_pass(step):
-        gather_up(step, below(step)).wait_recv()
-        if step < far - 1:
-            gather_up(step + 1, below(step)).start()
-            gather_mate(below(step), core).start()
-        gather_down(step, above(step)).wait_recv()
-        if step < far - 1:
-            gather_down(step + 1, above(step)).start()
-            gather_mate(above(step), core).start()
-        else:
-            gather_mate(above(step), core).start()
-
-    gather_up(0, z).start()
-    gather_down(0, z).start()
+        for way, chunk in ways:
+            if step < ring_steps(way, chunk):
+                block = gather_block(way, step)
+                gather_hop(way, chunk, step, block).wait_recv()
+                if step + 1 < ring_steps(way, chunk):
+                    gather_hop(way, chunk, step + 1, block).start()
+                gather_mate(chunk, block).start()
+
+    for way, chunk in ways:
+        if ring_steps(way, chunk) > 0:
+            gather_hop(way, chunk, 0, z).start()
 
     def block_to(peer):
         return remote(outgoing.at[peer], arrived.at[dp], b_send.at[0], b_recv.at[0], peer, z)
@@ -396,11 +392,8 @@
         ahead = (far if way == chunk else far - 1) - step
         return lax.rem(z + ahead, n.nz) if way == 0 else lax.rem(z + n.nz - ahead, n.nz)
 
-    def ring_steps(way, chunk):
-        return far if way == chunk else far - 1
-
     def ring_step(step):
-        for way, chunk in ((0, 0), (1, 1), (0, 1), (1, 0)):
+        for way, chunk in ways:
             if step < ring_steps(way, chunk):
                 out, into = (up_out, up_in) if way == 0 else (down_out, down_in)
                 value = part[ring_target(way, chunk, step), :, chunk_of[chunk]]
@@ -472,35 +465,11 @@
         kgrad[j // n.ltiles, pl.ds(at, TAPS), :] = jnp.sum(k8[...], axis=1)
         return carry
 
-    third = n.tiles // 3
-    lax.fori_loop(0, third, back_tile, 0)
-    if far > 1:
-        ring_step(1)
-    lax.fori_loop(third, n.tiles, back_tile, 0)
-    swap_k = remote(kgrad.at[other], mate_k, m_send.at[2], m_recv.at[2], mate, z)
-    swap_k.start()
-    if far > 2:
-        ring_step(2)
-
-    def gather_chunk(chunk, carry):
-        at = pl.ds(pl.multiple_of(chunk * chunk_rows, chunk_rows), chunk_rows)
-        total = None
-        for jj in range(4):
-            rhs = jnp.concatenate([go[4 * g + jj] for g in range(n.groups)], axis=1)
-            piece = dot(taking[jj, at, :], rhs)
-            total = piece if total is None else total + piece
-        for g in range(n.groups):
-            piece = total[:, 128 * g : 128 * (g + 1)].astype(BF16).reshape(per_chunk, 16, 128)
-            back[pl.ds(chunk * per_chunk, per_chunk), 16 * g : 16 * (g + 1), :] = piece
-        return carry
-
-    lax.fori_loop(0, lanes // chunk_rows, gather_chunk, 0)
-
-    def home_to(peer):
-        return remote(back.at[peer], home.at[dp], h_send.at[0], h_recv.at[0], peer, z)
-
-    swap_k.wait_recv()
-    mate_k[...] += kgrad[core]
+    def home_to(peer, group):
+        rows = pl.ds(16 * group, 16)
+        return remote(
+            back.at[peer, rows], home.at[dp, rows], h_send.at[group], h_recv.at[group], peer, z
+        )
 
     def k_rows(at):
         return pl.ds(pl.multiple_of(at * n.krow, 8), n.krow)
@@ -514,13 +483,33 @@
     def k_gather(slot, to):
         return remote(k_all.at[slot], k_all.at[slot], kc_send.at[0], kc_recv.at[0], 2 * to + core, z)
 
-    chips(lambda at: k_scatter(at, chip).start())
-
-    peers(lambda peer: home_to(peer).start())
+    swap_k = remote(kgrad.at[other], mate_k, m_send.at[2], m_recv.at[2], mate, z)
+    for group in range(n.groups):
+        lax.fori_loop(4 * group, 4 * group + 4, back_tile, 0)
+        if group == n.groups - 1:
+            swap_k.start()
+        if group + 1 < far:
+            ring_step(group + 1)
+
+        def gather_chunk(chunk, carry):
+            at = pl.ds(pl.multiple_of(chunk * chunk_rows, chunk_rows), chunk_rows)
+            total = dot(taking[0, at, :], go[4 * group])
+            for jj in range(1, 4):
+                total = total + dot(taking[jj, at, :], go[4 * group + jj])
+            piece = total.astype(BF16).reshape(per_chunk, 16, 128)
+            back[pl.ds(chunk * per_chunk, per_chunk), 16 * group : 16 * (group + 1), :] = piece
+            return carry
+
+        lax.fori_loop(0, lanes // chunk_rows, gather_chunk, 0)
+        if group == n.groups - 1:
+            swap_k.wait_recv()
+            mate_k[...] += kgrad[core]
+            chips(lambda at: k_scatter(at, chip).start())
+        peers(lambda peer: home_to(peer, group).start())
     home[dp] = back[dp]
 
 
-    for step in range(3, far):
+    for step in range(n.groups + 1, far):
         ring_step(step)
 
     await_bytes(k_in, n.chips - 1, ka_recv.at[0])
@@ -620,17 +609,17 @@
     swap_all = remote(k_all, k_mate, m_send.at[3], m_recv.at[3], mate, z)
     swap_all.start()
 
-    await_bytes(home, n.nd - 1, h_recv.at[0])
-    blocks = jnp.concatenate(
-        [home[:, 16 * g : 16 * (g + 1), :].reshape(lanes, 128) for g in range(n.groups)], axis=1
-    )
-    for jj in range(4):
-        rows = dot(unsort[n.rows * jj : n.rows * (jj + 1)], blocks).astype(BF16)
-        for g in range(n.groups):
-            frames_ref[:, 128 * (4 * g + jj) : 128 * (4 * g + jj + 1)] = rows[:, 128 * g : 128 * (g + 1)]
-    store = pltpu.make_async_copy(frames_ref, frames_out, io.at[3])
-    store.start()
-
+    def unsort_group(group):
+        rows = slice(16 * group, 16 * (group + 1))
+        await_bytes(home.at[:, pl.ds(16 * group, 16)], n.nd - 1, h_recv.at[group])
+        block = home[:, rows, :].reshape(lanes, 128)
+        for jj in range(4):
+            tile = 4 * group + jj
+            found = dot(unsort[n.rows * jj : n.rows * (jj + 1)], block).astype(BF16)
+            frames_ref[:, 128 * tile : 128 * (tile + 1)] = found
+
+    for group in range(n.groups - 1):
+        unsort_group(group)
     await_bytes(x_all, n.nx - 1, xg_recv.at[0])
     swap_weight = remote(x_all, x_mate, m_send.at[4], m_recv.at[4], mate, z)
     swap_weight.start()
@@ -644,10 +633,11 @@
         rows = source[...].reshape(n.kall, 128)
         for l in range(n.ltiles):
             cols = pl.ds(pl.multiple_of(half * n.half + 128 * l, 128), 128)
-            taps_out[:, cols] = rows[KROWS * l : KROWS * l + TAPS]
-            gain_out[cols] = rows[KROWS * l + TAPS : KROWS * l + TAPS + 1].reshape(128)
-            shift_out[cols] = rows[KROWS * l + TAPS + 1 : KROWS * l + TAPS + 2].reshape(128)
-
+            small_out[:, cols] = rows[KROWS * l : KROWS * (l + 1)]
+
+    unsort_group(n.groups - 1)
+    store = pltpu.make_async_copy(frames_ref, frames_out, io.at[3])
+    store.start()
     lay_weight(x_all, core)
     lay_small(k_all, core)
 
@@ -659,8 +649,9 @@
     for copy in (swap_cot, swap_act, swap_k, swap_all, swap_weight):
         copy.wait_send()
     for step in range(far):
-        gather_up(step, z).wait_send()
-        gather_down(step, z).wait_send()
+        for way, chunk in ways:
+            if step < ring_steps(way, chunk):
+                gather_hop(way, chunk, step, z).wait_send()
     for way in range(2):
         for chunk in range(2):
             for step in range(ring_steps(way, chunk)):
@@ -679,8 +670,40 @@
     await_bytes(k_all, n.chips - 1, kc_send.at[0])
     await_bytes(label_out, n.nd - 1, l_send.at[0])
     await_bytes(outgoing, n.nd - 1, b_send.at[0])
-    await_bytes(back, n.nd - 1, h_send.at[0])
+    for group in range(n.groups):
+        await_bytes(back.at[:, pl.ds(16 * group, 16)], n.nd - 1, h_send.at[group])
     store.wait()
+
+
+def finish_kernel(n, frames_ref, weight_ref, small_ref, frames_out, weight_out, taps_out, gain_out, shift_out):
+    frames_out[...] = frames_ref[...]
+    weight_out[...] = weight_ref[...].astype(F32)
+
+    @pl.when(pl.program_id(0) == 0)
+    def _():
+        taps_out[...] = small_ref[:TAPS]
+        gain_out[...] = small_ref[TAPS : TAPS + 1].reshape(n.ch)
+        shift_out[...] = small_ref[TAPS + 1 : TAPS + 2].reshape(n.ch)
+
+
+def finish(n, frames, weight, small):
+    steps = 4
+    band = pl.BlockSpec((n.rows // steps, n.ch), lambda i: (i, 0))
+    shard = pl.BlockSpec((n.shard // steps, n.ch), lambda i: (i, 0))
+    vector = pl.BlockSpec((n.ch,), lambda i: (0,))
+    return pl.pallas_call(
+        functools.partial(finish_kernel, n),
+        grid=(steps,),
+        out_shape=(
+            jax.ShapeDtypeStruct((n.rows, n.ch), BF16),
+            jax.ShapeDtypeStruct((n.shard, n.ch), F32),
+            jax.ShapeDtypeStruct((TAPS, n.ch), F32),
+            jax.ShapeDtypeStruct((n.ch,), F32),
+            jax.ShapeDtypeStruct((n.ch,), F32),
+        ),
+        in_specs=[band, shard, pl.BlockSpec((KROWS, n.ch), lambda i: (0, 0))],
+        out_specs=(band, shard, pl.BlockSpec((TAPS, n.ch), lambda i: (0, 0)), vector, vector),
+    )(frames, weight, small)
 
 
 def on_device(frames, destination, utt_lengths, cotangent, weight, kernel, norm_gain, norm_shift):
@@ -710,12 +733,10 @@
         out_shape=(
             jax.ShapeDtypeStruct((n.rows, n.ch), BF16),
             jax.ShapeDtypeStruct((n.shard, n.ch), BF16),
-            jax.ShapeDtypeStruct((TAPS, n.ch), F32),
-            jax.ShapeDtypeStruct((n.ch,), F32),
-            jax.ShapeDtypeStruct((n.ch,), F32),
+            jax.ShapeDtypeStruct((KROWS, n.ch), F32),
         ),
         in_specs=[vmem, smem, hbm, hbm, hbm, vmem, vmem, vmem],
-        out_specs=(hbm, vmem, vmem, vmem, vmem),
+        out_specs=(hbm, vmem, vmem),
         scratch_shapes=[
             buf(n.rows, n.ch, dtype=BF16), buf(n.rows, n.ch, dtype=BF16),
             blocks, blocks, label, label, buf(16 * n.nb, 128), buf(n.nz, n.shard, n.ch, dtype=BF16),
@@ -727,8 +748,8 @@
             buf(n.nz, n.shard, n.half), ring, ring, ring, ring, blocks, blocks,
             band, band, buf(n.ltiles, n.prow, 128), tile, tile, tile, band, band,
             buf(n.kall, 128), small, buf(n.nz, n.krow, 128), small, small,
-            pltpu.SemaphoreType.DMA((4,)), *dma(1), *dma(1), *dma(1),
-            *dma(far), *dma(far), *dma(1), *dma(5),
+            pltpu.SemaphoreType.DMA((4,)), *dma(1), *dma(1), *dma(n.groups),
+            *dma(2 * far), *dma(2 * far), *dma(1), *dma(5),
             *dma(2 * far), *dma(2 * far),
             *dma(1), *dma(1), *dma(1), *dma(1),
             *dma(1), *dma(1), *dma(1),
@@ -737,7 +758,7 @@
             collective_id=0, has_side_effects=True, vmem_limit_bytes=VMEM_BYTES
         ),
     )(destination, utt_lengths, frames, cotangent, weight, kernel, norm_gain, norm_shift)
-    return grads[0], grads[1].astype(F32), grads[2], grads[3], grads[4]
+    return finish(n, *grads)
 
 
 def solution(mesh):

time: 124 us -> 121 us (0.976)
  local copies, waits for them, and re-layouts: 2.97 us -> 0 us
  other arithmetic: 2.28 us -> 0 us
  Pallas kernels: 118 us -> 120 us
    pallas_call x0 -> x1, Pallas kernels: none -> 3.88 us  [finish(): pl.pallas_call(functools.partial(finish_kernel, n), grid=(steps,), out_sh...]
    unnamed x12 -> x0, local copies, waits for them, and re-layouts: 2.97 us -> none
    convert_element_type x1 -> x0, other arithmetic: 2.28 us -> none  [on_device(): return (grads[0], grads[1].astype(F32), grads[2], grads[3], grads[4])]
    pallas_call x1, Pallas kernels: 118 us -> 116 us  [on_device(): pl.pallas_call(functools.partial(module_kernel, n, scale), out_shape=(jax...]
where the time goes in v5:
time: 121 us; the launch traced here: 120 us
  Pallas kernels  120 us (99%)
    pallas_call x1, Pallas kernels, on_device(): pl.pallas_call(functools.partial(module_kernel, n, scale), out_shape=(jax...  116 us
    pallas_call x1, Pallas kernels, finish(): pl.pallas_call(functools.partial(finish_kernel, n), grid=(steps,), out_sh...  3.88 us

profile of v5, /device:TPU:1, one launch (start us, length us, event | category | flops | bytes accessed | tf_op | source)
XLA Modules:
  0.0 120.3 jit_solution(10496913349762416408)
XLA Ops:
  0.6 115.6 %shard_map.119 = (bf16[256,1536]{1,0:T(8,128)(2,1)}, bf16[192,1536]{1,0:T(8,128)(2,1)}, f32[40,1536]{1,0:T(8,128)}) custom-call(s32[64]{0:T(128)} %dest_ref.1, s32[1,4]{1,0:T(1,128)} %utt_ref.1, bf16[256,1536]{1,0:T(8,128)(2,1)} %frames_hbm.1, bf16[256,1536]{1,0:T(8,128)(2,1)} %cot_hbm.1, bf16[192,1536]{1,0:T(8,128)(2,1)} %weight_hbm.1, ...), custom_call_target="tpu_custom_call" | custom-call | tf_op jit(solution)/shard_map/pallas_call | solution.py:731
  116.3 3.9 %shard_map.120 = (bf16[256,1536]{1,0:T(8,128)(2,1)}, f32[192,1536]{1,0:T(8,128)}, f32[31,1536]{1,0:T(8,128)}, f32[1536]{0:T(1024)}, f32[1536]{0:T(1024)}) custom-call(bf16[256,1536]{1,0:T(8,128)(2,1)} %get-tuple-element.8.frames_ref, bf16[192,1536]{1,0:T(8,128)(2,1)} %get-tuple-element.9.weight_ref, f32[40,1536]{1,0:T(8,128)} %get-tuple-element.10.small_ref), custom_call_target="tpu_custom_call" | custom-call | tf_op jit(solution)/shard_map/pallas_call | solution.py:694

commit v6 on v5

--- a/solution.py
+++ b/solution.py
@@ -327,7 +327,6 @@
         return carry
 
     lax.fori_loop(0, n.tiles, filter_tile, 0)
-    gather_pass(far - 1)
 
     def norm_span(b, carry):
         rows = pl.ds(pl.multiple_of(HALO + n.span * b, 16), n.span)
@@ -361,23 +360,12 @@
     swap_act.start()
     act_both[: n.rows] = dot(take, actp[:, mine]).astype(BF16)
 
-    await_bytes(whole.at[:, pl.ds(0, hrow)], n.nz - 1, gm_recv.at[0])
-    width = 512
-    per = width // 128
-
-    def project(i, carry):
-        cols = pl.ds(pl.multiple_of(i * width, width), width)
-        piece = dot(cot_pad[...], whole[:, :, cols].reshape(n.ch, width))
-        for q in range(per):
-            hidden[per * i + q] = piece[:, 128 * q : 128 * (q + 1)]
-        return carry
-
-    lax.fori_loop(0, n.ch // width, project, 0)
-
-    swap_act.wait_recv()
-
     def product(target):
         part[target] = dot(cot_turned[pl.ds(pl.multiple_of(target * n.shard, 16), n.shard), :], act_both[...])
+
+    def product_of(target, core_rows):
+        rows = pl.ds(pl.multiple_of(target * n.shard, 16), n.shard)
+        return dot(cot_turned[rows, core_rows], act_both[core_rows, :])
 
     chunk_of = [slice(0, n.quarter), slice(n.quarter, n.half)]
 
@@ -403,11 +391,29 @@
                 out[chunk, step] = value.astype(BF16)
                 ring_hop(way, chunk, step).start()
 
-    product(lax.rem(z + far, n.nz))
+    first = [lax.rem(z + far, n.nz)]
     if far > 1:
-        product(lax.rem(z + far - 1, n.nz))
-        product(lax.rem(z + n.nz - far + 1, n.nz))
+        first += [lax.rem(z + far - 1, n.nz), lax.rem(z + n.nz - far + 1, n.nz)]
+    for target in first:
+        part[target] = product_of(target, slice(0, n.rows))
+    swap_act.wait_recv()
+    for target in first:
+        part[target] += product_of(target, slice(n.rows, 2 * n.rows))
     ring_step(0)
+
+    gather_pass(far - 1)
+    await_bytes(whole.at[:, pl.ds(0, hrow)], n.nz - 1, gm_recv.at[0])
+    width = 512
+    per = width // 128
+
+    def project(i, carry):
+        cols = pl.ds(pl.multiple_of(i * width, width), width)
+        piece = dot(cot_pad[...], whole[:, :, cols].reshape(n.ch, width))
+        for q in range(per):
+            hidden[per * i + q] = piece[:, 128 * q : 128 * (q + 1)]
+        return carry
+
+    lax.fori_loop(0, n.ch // width, project, 0)
 
     def norm_back(b, carry):
         rows = pl.ds(pl.multiple_of(HALO + n.span * b, 16), n.span)
@@ -675,25 +681,23 @@
     store.wait()
 
 
-def finish_kernel(n, frames_ref, weight_ref, small_ref, frames_out, weight_out, taps_out, gain_out, shift_out):
-    frames_out[...] = frames_ref[...]
+def finish_kernel(
+    n, frames_hbm, weight_ref, small_ref, frames_out, weight_out, taps_out, gain_out, shift_out, sem
+):
+    copy = pltpu.make_async_copy(frames_hbm, frames_out, sem)
+    copy.start()
     weight_out[...] = weight_ref[...].astype(F32)
-
-    @pl.when(pl.program_id(0) == 0)
-    def _():
-        taps_out[...] = small_ref[:TAPS]
-        gain_out[...] = small_ref[TAPS : TAPS + 1].reshape(n.ch)
-        shift_out[...] = small_ref[TAPS + 1 : TAPS + 2].reshape(n.ch)
+    taps_out[...] = small_ref[:TAPS]
+    gain_out[...] = small_ref[TAPS : TAPS + 1].reshape(n.ch)
+    shift_out[...] = small_ref[TAPS + 1 : TAPS + 2].reshape(n.ch)
+    copy.wait()
 
 
 def finish(n, frames, weight, small):
-    steps = 4
-    band = pl.BlockSpec((n.rows // steps, n.ch), lambda i: (i, 0))
-    shard = pl.BlockSpec((n.shard // steps, n.ch), lambda i: (i, 0))
-    vector = pl.BlockSpec((n.ch,), lambda i: (0,))
+    vmem = pl.BlockSpec(memory_space=pltpu.VMEM)
+    hbm = pl.BlockSpec(memory_space=pl.ANY)
     return pl.pallas_call(
         functools.partial(finish_kernel, n),
-        grid=(steps,),
         out_shape=(
             jax.ShapeDtypeStruct((n.rows, n.ch), BF16),
             jax.ShapeDtypeStruct((n.shard, n.ch), F32),
@@ -701,8 +705,9 @@
             jax.ShapeDtypeStruct((n.ch,), F32),
             jax.ShapeDtypeStruct((n.ch,), F32),
         ),
-        in_specs=[band, shard, pl.BlockSpec((KROWS, n.ch), lambda i: (0, 0))],
-        out_specs=(band, shard, pl.BlockSpec((TAPS, n.ch), lambda i: (0, 0)), vector, vector),
+        in_specs=[hbm, vmem, vmem],
+        out_specs=(hbm, vmem, vmem, vmem, vmem),
+        scratch_shapes=[pltpu.SemaphoreType.DMA],
     )(frames, weight, small)
 
 

time: 121 us -> 145 us (1.20)
  Pallas kernels: 120 us -> 144 us
    pallas_call x1, Pallas kernels: 3.88 us -> 27.1 us  [finish(): pl.pallas_call(functools.partial(finish_kernel, n), out_shape=(jax.ShapeD...]
where the time goes in v6:
time: 145 us
  Pallas kernels  144 us (99%)
    pallas_call x1, Pallas kernels, on_device(): pl.pallas_call(functools.partial(module_kernel, n, scale), out_shape=(jax...  117 us
    pallas_call x1, Pallas kernels, finish(): pl.pallas_call(functools.partial(finish_kernel, n), out_shape=(jax.ShapeD...  27.1 us

profile of v6, /device:TPU:1, one launch (start us, length us, event | category | flops | bytes accessed | tf_op | source)
XLA Modules:
  0.0 145.0 jit_solution(6189635905774933857)
XLA Ops:
  0.6 117.0 %shard_map.119 = (bf16[256,1536]{1,0:T(8,128)(2,1)}, bf16[192,1536]{1,0:T(8,128)(2,1)}, f32[40,1536]{1,0:T(8,128)}) custom-call(s32[64]{0:T(128)} %dest_ref.1, s32[1,4]{1,0:T(1,128)} %utt_ref.1, bf16[256,1536]{1,0:T(8,128)(2,1)} %frames_hbm.1, bf16[256,1536]{1,0:T(8,128)(2,1)} %cot_hbm.1, bf16[192,1536]{1,0:T(8,128)(2,1)} %weight_hbm.1, ...), custom_call_target="tpu_custom_call" | custom-call | tf_op jit(solution)/shard_map/pallas_call | solution.py:736
  117.7 27.1 %shard_map.120 = (bf16[256,1536]{1,0:T(8,128)(2,1)}, f32[192,1536]{1,0:T(8,128)}, f32[31,1536]{1,0:T(8,128)}, f32[1536]{0:T(1024)}, f32[1536]{0:T(1024)}) custom-call(bf16[256,1536]{1,0:T(8,128)(2,1)} %get-tuple-element.8.frames_hbm, bf16[192,1536]{1,0:T(8,128)(2,1)} %get-tuple-element.9.weight_ref, f32[40,1536]{1,0:T(8,128)} %get-tuple-element.10.small_ref), custom_call_target="tpu_custom_call" | custom-call | tf_op jit(solution)/shard_map/pallas_call | solution.py:699

commit v7 on v5

--- a/solution.py
+++ b/solution.py
@@ -512,16 +512,6 @@
     for step in range(n.groups + 1, far):
         ring_step(step)
 
-    await_bytes(k_in, n.chips - 1, ka_recv.at[0])
-    k_in[chip] = mate_k[k_rows(chip), :]
-
-    def k_sum(step, carry):
-        return carry + k_in[lax.rem(chip + step, n.chips)]
-
-    k_z[z] = lax.fori_loop(1, n.chips, k_sum, k_in[chip])
-    for hop in range(1, n.nz):
-        k_over_z(z, lax.rem(z + hop, n.nz)).start()
-
     for way, chunk in ((1, 0), (0, 1), (0, 0), (1, 1)):
         steps = ring_steps(way, chunk)
         if steps > 0:
@@ -558,12 +548,15 @@
     for step in range(1, n.nx):
         x_scatter(step).start()
 
-    await_bytes(k_z, n.nz - 1, kz_recv.at[0])
-    small = k_z[0]
-    for i in range(1, n.nz):
-        small = small + k_z[i]
-    k_all[chip] = small * scale
-    chips(lambda at: k_gather(chip, at).start())
+    await_bytes(k_in, n.chips - 1, ka_recv.at[0])
+    k_in[chip] = mate_k[k_rows(chip), :]
+
+    def k_sum(step, carry):
+        return carry + k_in[lax.rem(chip + step, n.chips)]
+
+    k_z[z] = lax.fori_loop(1, n.chips, k_sum, k_in[chip])
+    for hop in range(1, n.nz):
+        k_over_z(z, lax.rem(z + hop, n.nz)).start()
 
     band = part[z, pl.ds(pl.multiple_of(cx * n.prow, 16), n.prow), :]
     await_bytes(x_in, n.nx - 1, xr_recv.at[0])
@@ -579,6 +572,13 @@
         def _():
             copy.start()
 
+    await_bytes(k_z, n.nz - 1, kz_recv.at[0])
+    small = k_z[0]
+    for i in range(1, n.nz):
+        small = small + k_z[i]
+    k_all[chip] = small * scale
+    chips(lambda at: k_gather(chip, at).start())
+
     @pl.when(cy < n.ltiles)
     def _():
         await_bytes(y_in, n.ny - 1, yr_recv.at[0])
@@ -605,10 +605,6 @@
     for step in range(1, n.nx):
         x_gather(step).start()
 
-    await_bytes(k_all, n.chips - 1, kc_recv.at[0])
-    swap_all = remote(k_all, k_mate, m_send.at[3], m_recv.at[3], mate, z)
-    swap_all.start()
-
     def unsort_group(group):
         rows = slice(16 * group, 16 * (group + 1))
         await_bytes(home.at[:, pl.ds(16 * group, 16)], n.nd - 1, h_recv.at[group])
@@ -623,6 +619,10 @@
     await_bytes(x_all, n.nx - 1, xg_recv.at[0])
     swap_weight = remote(x_all, x_mate, m_send.at[4], m_recv.at[4], mate, z)
     swap_weight.start()
+
+    await_bytes(k_all, n.chips - 1, kc_recv.at[0])
+    swap_all = remote(k_all, k_mate, m_send.at[3], m_recv.at[3], mate, z)
+    swap_all.start()
 
     def lay_weight(source, half):
         cols = pl.ds(pl.multiple_of(half * n.half, 128), n.half)
@@ -678,22 +678,15 @@
 def finish_kernel(n, frames_ref, weight_ref, small_ref, frames_out, weight_out, taps_out, gain_out, shift_out):
     frames_out[...] = frames_ref[...]
     weight_out[...] = weight_ref[...].astype(F32)
-
-    @pl.when(pl.program_id(0) == 0)
-    def _():
-        taps_out[...] = small_ref[:TAPS]
-        gain_out[...] = small_ref[TAPS : TAPS + 1].reshape(n.ch)
-        shift_out[...] = small_ref[TAPS + 1 : TAPS + 2].reshape(n.ch)
+    taps_out[...] = small_ref[:TAPS]
+    gain_out[...] = small_ref[TAPS : TAPS + 1].reshape(n.ch)
+    shift_out[...] = small_ref[TAPS + 1 : TAPS + 2].reshape(n.ch)
 
 
 def finish(n, frames, weight, small):
-    steps = 4
-    band = pl.BlockSpec((n.rows // steps, n.ch), lambda i: (i, 0))
-    shard = pl.BlockSpec((n.shard // steps, n.ch), lambda i: (i, 0))
-    vector = pl.BlockSpec((n.ch,), lambda i: (0,))
+    vmem = pl.BlockSpec(memory_space=pltpu.VMEM)
     return pl.pallas_call(
         functools.partial(finish_kernel, n),
-        grid=(steps,),
         out_shape=(
             jax.ShapeDtypeStruct((n.rows, n.ch), BF16),
             jax.ShapeDtypeStruct((n.shard, n.ch), F32),
@@ -701,8 +694,9 @@
             jax.ShapeDtypeStruct((n.ch,), F32),
             jax.ShapeDtypeStruct((n.ch,), F32),
         ),
-        in_specs=[band, shard, pl.BlockSpec((KROWS, n.ch), lambda i: (0, 0))],
-        out_specs=(band, shard, pl.BlockSpec((TAPS, n.ch), lambda i: (0, 0)), vector, vector),
+        in_specs=[vmem] * 3,
+        out_specs=(vmem,) * 5,
+        compiler_params=pltpu.CompilerParams(vmem_limit_bytes=16 * 1024 * 1024),
     )(frames, weight, small)
 
 

time: 121 us -> 117 us (0.967)
  Pallas kernels: 120 us -> 113 us
  local copies, waits for them, and re-layouts: 0 us -> 3.13 us
    pallas_call x1, Pallas kernels: 116 us -> 111 us  [on_device(): pl.pallas_call(functools.partial(module_kernel, n, scale), out_shape=(jax...]
    unnamed x0 -> x6, local copies, waits for them, and re-layouts: none -> 3.13 us
    pallas_call x1, Pallas kernels: 3.88 us -> 1.45 us  [finish(): pl.pallas_call(functools.partial(finish_kernel, n), out_shape=(jax.ShapeD...]
where the time goes in v7:
time: 117 us
  Pallas kernels  113 us (97%)
  local copies, waits for them, and re-layouts  3.13 us (3%)
    pallas_call x1, Pallas kernels, on_device(): pl.pallas_call(functools.partial(module_kernel, n, scale), out_shape=(jax...  111 us
    unnamed x6, local copies, waits for them, and re-layouts  3.13 us

profile of v7, /device:TPU:1, one launch (start us, length us, event | category | flops | bytes accessed | tf_op | source)
XLA Modules:
  0.0 116.5 jit_solution(8325170589511975978)
XLA Ops:
  0.6 111.3 %shard_map.119 = (bf16[256,1536]{1,0:T(8,128)(2,1)}, bf16[192,1536]{1,0:T(8,128)(2,1)}, f32[40,1536]{1,0:T(8,128)}) custom-call(s32[64]{0:T(128)} %dest_ref.1, s32[1,4]{1,0:T(1,128)} %utt_ref.1, bf16[256,1536]{1,0:T(8,128)(2,1)} %frames_hbm.1, bf16[256,1536]{1,0:T(8,128)(2,1)} %cot_hbm.1, bf16[192,1536]{1,0:T(8,128)(2,1)} %weight_hbm.1, ...), custom_call_target="tpu_custom_call" | custom-call | tf_op jit(solution)/shard_map/pallas_call | solution.py:725
  111.9 0.0 copy-start
  111.9 1.1 copy-done
  113.1 0.0 copy-start.1
  113.1 1.1 copy-done.1
  114.1 0.0 copy-start.2
  114.1 0.9 copy-done.2
  115.1 1.5 %shard_map.120 = (bf16[256,1536]{1,0:T(8,128)(2,1)}, f32[192,1536]{1,0:T(8,128)}, f32[31,1536]{1,0:T(8,128)}, f32[1536]{0:T(1024)}, f32[1536]{0:T(1024)}) custom-call(bf16[256,1536]{1,0:T(8,128)(2,1)S(1)} %copy-done, bf16[192,1536]{1,0:T(8,128)(2,1)S(1)} %copy-done.1, f32[40,1536]{1,0:T(8,128)S(1)} %copy-done.2), custom_call_target="tpu_custom_call" | custom-call | tf_op jit(solution)/shard_map/pallas_call | solution.py:688
Async XLA Ops:
  111.9 1.1 copy-start
  113.1 1.1 copy-start.1
  114.1 0.9 copy-start.2
